TPU v7x, 32 devices: a whole 2x2x4 slice. The times are simulated.
32 devices in a mesh: dp: 8 (over z, x), mp: 4 (over y, core).
Axes of the slice: x: 2, y: 2, z: 4, core: 2. Of those that a mesh axis runs over, the one named last changes fastest.
Arguments:
- tokens: bfloat16 [2048, 1024], P('dp'), may hold values from -6 to 6
- segment_ids: int32 [8, 256], P('dp'), may hold values from 0 to 7, never falling along the last dimension, each value on 1 to 128 neighbouring positions
- attn_gain: float32 [1024], replicated, may hold values from 0.5 to 1.5
- w_query: bfloat16 [1024, 1024], P(None, 'mp'), may hold values from -0.1875 to 0.1875
- w_key: bfloat16 [1024, 512], P(None, 'mp'), may hold values from -0.1875 to 0.1875
- w_value: bfloat16 [1024, 512], P(None, 'mp'), may hold values from -0.1875 to 0.1875
- query_gain: float32 [64], replicated, may hold values from 0.6 to 1.4, as said below
- key_gain: float32 [64], replicated, may hold values from 0.6 to 1.4, as said below
- w_out: bfloat16 [1024, 1024], P('mp'), may hold values from -0.75 to 0.75
- ffn_gain: float32 [1024], replicated, may hold values from 0.5 to 1.5
- w_gate: bfloat16 [1024, 4608], P('dp', 'mp'), may hold values from -0.1875 to 0.1875
- w_up: bfloat16 [1024, 4608], P('dp', 'mp'), may hold values from -0.1875 to 0.1875
- w_down: bfloat16 [4608, 1024], P('mp', 'dp'), may hold values from -0.375 to 0.375
- grad_out: bfloat16 [2048, 1024], P('dp'), may hold values from -6 to 6
Outputs:
- output: bfloat16 [2048, 1024], P('dp')
- grad_tokens: float32 [2048, 1024], P('dp')
- grad_attn_gain: float32 [1024], replicated
- grad_w_query: float32 [1024, 1024], P(None, 'mp')
- grad_w_key: float32 [1024, 512], P(None, 'mp')
- grad_w_value: float32 [1024, 512], P(None, 'mp')
- grad_query_gain: float32 [64], replicated
- grad_key_gain: float32 [64], replicated
- grad_w_out: float32 [1024, 1024], P('mp')
- grad_ffn_gain: float32 [1024], replicated
- grad_w_gate: float32 [1024, 4608], P('dp', 'mp')
- grad_w_up: float32 [1024, 4608], P('dp', 'mp')
- grad_w_down: float32 [4608, 1024], P('mp', 'dp')
Inputs may be any that keep to these rules, and one draw needn't show every extreme that they name: `segment_ids`: within one row the ids never fall; each row holds 8 sequences, each a run of 1 to 128 tokens, and some run has exactly 128. `query_gain`: positive scales. `key_gain`: positive scales.
All inputs are finite; a program needn't handle non-finite values.
Results may differ from a plain program's by a relative error of at most 0.015.
Values may be sent and summed in bfloat16 or wider, within the bound.
A program may use at most 128 MiB of HBM per device.

v0:
```python
import math

import jax
import jax.numpy as jnp
from jax import lax
from jax.sharding import PartitionSpec as P

HEAD_DIM = 64


EPS = 1e-05
ROPE_BASE = 1000000.0


def rms_scale(values):
    return lax.rsqrt(jnp.mean(values * values, axis=-1, keepdims=True) + EPS)


def norm_back(values, scale_fac, gain_vec, grad_normed):
    weighted = grad_normed * gain_vec
    grad_values = scale_fac * weighted - values * scale_fac * scale_fac * scale_fac * jnp.mean(
        weighted * values, axis=-1, keepdims=True
    )
    grad_gain = jnp.sum((grad_normed * values * scale_fac).reshape(-1, values.shape[-1]), axis=0)
    return (grad_values, grad_gain)


def segment_layout(segment_row):
    token_count = segment_row.shape[0]
    token_index = jnp.arange(token_count, dtype=jnp.int32)
    same_doc = segment_row[:, None] == segment_row[None, :]
    starts = jnp.min(jnp.where(same_doc, token_index[None, :], token_count), axis=1)
    allowed = same_doc & (token_index[None, :] <= token_index[:, None])
    return ((token_index - starts).astype(jnp.float32), allowed)


def rotary_tables(position, head_width):
    half_index = jnp.arange(head_width // 2, dtype=jnp.float32)
    frequency = ROPE_BASE ** (-2.0 * half_index / head_width)
    angles = position[:, None] * frequency[None, :]
    return (jnp.cos(angles)[:, None, :], jnp.sin(angles)[:, None, :])


def rotate(values, cosine, sine_table):
    half_width = values.shape[-1] // 2
    front_part = values[..., :half_width]
    back_part = values[..., half_width:]
    return jnp.concatenate(
        [
            front_part * cosine - back_part * sine_table,
            back_part * cosine + front_part * sine_table,
        ],
        axis=-1,
    )


def rotate_back(grads_in, cosine, sine_table):
    half_width = grads_in.shape[-1] // 2
    front_part = grads_in[..., :half_width]
    back_part = grads_in[..., half_width:]
    return jnp.concatenate(
        [
            front_part * cosine + back_part * sine_table,
            back_part * cosine - front_part * sine_table,
        ],
        axis=-1,
    )


def masked_scores(query_rot, key_rot, allowed):
    token_count, head_count, head_width = query_rot.shape
    group_count = key_rot.shape[1]
    grouped = query_rot.reshape(token_count, group_count, head_count // group_count, head_width)
    scores = jnp.einsum("qgrd,kgd->grqk", grouped, key_rot, preferred_element_type=jnp.float32) * (
        1.0 / math.sqrt(head_width)
    )
    return (jnp.where(allowed, scores, -1e30), grouped)


def attention_forward(query_rot, key_rot, value_half, allowed):
    token_count, head_count, head_width = query_rot.shape
    scores, grouped = masked_scores(query_rot, key_rot, allowed)
    row_peak = jnp.max(scores, axis=-1, keepdims=True)
    raised = jnp.exp(scores - row_peak)
    row_total = jnp.sum(raised, axis=-1, keepdims=True)
    logsum = row_peak + jnp.log(row_total)
    prob_half = (raised / row_total).astype(jnp.bfloat16)
    attended = jnp.einsum(
        "grqk,kgd->qgrd", prob_half, value_half, preferred_element_type=jnp.float32
    ).astype(jnp.bfloat16)
    return (attended.reshape(token_count, head_count, head_width), logsum)


def attention_backward(query_rot, key_rot, value_half, allowed, attended, logsum, d_attended):
    token_count, head_count, head_width = query_rot.shape
    group_count = key_rot.shape[1]
    scores, grouped = masked_scores(query_rot, key_rot, allowed)
    probs = jnp.where(allowed, jnp.exp(scores - logsum), 0.0)
    prob_half = probs.astype(jnp.bfloat16)
    d_grouped = d_attended.reshape(token_count, group_count, head_count // group_count, head_width)
    d_value = jnp.einsum(
        "grqk,qgrd->kgd", prob_half, d_grouped, preferred_element_type=jnp.float32
    ).astype(jnp.bfloat16)
    d_probs = jnp.einsum(
        "qgrd,kgd->grqk", d_grouped, value_half, preferred_element_type=jnp.float32
    )
    row_delta = jnp.sum(d_attended.astype(jnp.float32) * attended.astype(jnp.float32), axis=-1)
    row_delta = row_delta.reshape(token_count, group_count, head_count // group_count).transpose(
        1, 2, 0
    )[..., None]
    d_scores = (probs * (d_probs - row_delta) * (1.0 / math.sqrt(head_width))).astype(jnp.bfloat16)
    d_query_rot = jnp.einsum(
        "grqk,kgd->qgrd", d_scores, key_rot, preferred_element_type=jnp.float32
    ).reshape(token_count, head_count, head_width)
    d_key_rot = jnp.einsum("grqk,qgrd->kgd", d_scores, grouped, preferred_element_type=jnp.float32)
    return (d_query_rot, d_key_rot, d_value)


def shards(
    tokens,
    segment_ids,
    attn_gain,
    w_query,
    w_key,
    w_value,
    query_gain,
    key_gain,
    w_out,
    ffn_gain,
    w_gate,
    w_up,
    w_down,
    grad_out,
):
    token_count = tokens.shape[0]
    mid_width = w_gate.shape[1]
    across = (((1,), (1,)), ((), ()))
    down_rows = (((0,), (0,)), ((), ()))
    inputs = tokens.astype(jnp.float32)
    scale_in = rms_scale(inputs)
    normed_in = (inputs * scale_in * attn_gain).astype(jnp.bfloat16)
    query_proj = jnp.dot(normed_in, w_query, preferred_element_type=jnp.float32).reshape(
        token_count, -1, HEAD_DIM
    )
    key_proj = jnp.dot(normed_in, w_key, preferred_element_type=jnp.float32).reshape(
        token_count, -1, HEAD_DIM
    )
    value_half = (
        jnp.dot(normed_in, w_value, preferred_element_type=jnp.float32)
        .astype(jnp.bfloat16)
        .reshape(token_count, -1, HEAD_DIM)
    )
    query_scale = rms_scale(query_proj)
    key_scale = rms_scale(key_proj)
    position, allowed = segment_layout(segment_ids[0])
    cosine, sine_table = rotary_tables(position, HEAD_DIM)
    query_rot = rotate(query_proj * query_scale * query_gain, cosine, sine_table).astype(
        jnp.bfloat16
    )
    key_rot = rotate(key_proj * key_scale * key_gain, cosine, sine_table).astype(jnp.bfloat16)
    attended, logsum = attention_forward(query_rot, key_rot, value_half, allowed)
    attn_flat = attended.reshape(token_count, -1)
    head_part = jnp.dot(attn_flat, w_out, preferred_element_type=jnp.float32)
    hidden = inputs + lax.psum(head_part, "mp")
    scale_mid = rms_scale(hidden)
    normed_mid = (hidden * scale_mid * ffn_gain).astype(jnp.bfloat16)
    pieces = (
        lax.all_gather(w_gate, "dp", axis=0, tiled=True),
        lax.all_gather(w_up, "dp", axis=0, tiled=True),
    )
    columns = normed_mid
    gate_proj = jnp.dot(columns, pieces[0], preferred_element_type=jnp.float32)
    up_proj = jnp.dot(columns, pieces[1], preferred_element_type=jnp.float32)
    sig_gate = jax.nn.sigmoid(gate_proj)
    activated = (gate_proj * sig_gate * up_proj).astype(jnp.bfloat16)
    ffn_part = jnp.dot(
        activated,
        lax.all_gather(w_down, "dp", axis=1, tiled=True),
        preferred_element_type=jnp.float32,
    )
    output = (hidden + lax.psum(ffn_part, "mp")).astype(jnp.bfloat16)
    columns = grad_out
    d_act = lax.dot_general(
        columns,
        lax.all_gather(w_down, "dp", axis=1, tiled=True),
        across,
        preferred_element_type=jnp.float32,
    )
    d_up = (d_act * gate_proj * sig_gate).astype(jnp.bfloat16)
    d_gate = (d_act * up_proj * sig_gate * (1.0 + gate_proj * (1.0 - sig_gate))).astype(
        jnp.bfloat16
    )
    pieces = lax.all_gather((w_gate, w_up), "dp", axis=0, tiled=True)
    d_mid_part = lax.dot_general(
        d_gate, pieces[0], across, preferred_element_type=jnp.float32
    ) + lax.dot_general(d_up, pieces[1], across, preferred_element_type=jnp.float32)
    d_mid = lax.psum(d_mid_part, "mp")
    d_hidden_norm, g_ffn_gain = norm_back(hidden, scale_mid, ffn_gain, d_mid)
    d_hidden = grad_out.astype(jnp.float32) + d_hidden_norm
    d_hidden_half = d_hidden.astype(jnp.bfloat16)
    g_out = lax.dot_general(attn_flat, d_hidden_half, down_rows, preferred_element_type=jnp.float32)
    d_attended = (
        lax.dot_general(d_hidden_half, w_out, across, preferred_element_type=jnp.float32)
        .astype(jnp.bfloat16)
        .reshape(token_count, -1, HEAD_DIM)
    )
    d_query_rot, d_key_rot, d_value = attention_backward(
        query_rot, key_rot, value_half, allowed, attended, logsum, d_attended
    )
    d_query, g_query_part = norm_back(
        query_proj, query_scale, query_gain, rotate_back(d_query_rot, cosine, sine_table)
    )
    d_key, g_key_part = norm_back(
        key_proj, key_scale, key_gain, rotate_back(d_key_rot, cosine, sine_table)
    )
    d_query_half = d_query.astype(jnp.bfloat16).reshape(token_count, -1)
    d_key_half = d_key.astype(jnp.bfloat16).reshape(token_count, -1)
    d_value_half = d_value.reshape(token_count, -1)
    g_query = lax.dot_general(
        normed_in, d_query_half, down_rows, preferred_element_type=jnp.float32
    )
    g_key = lax.dot_general(normed_in, d_key_half, down_rows, preferred_element_type=jnp.float32)
    g_value = lax.dot_general(
        normed_in, d_value_half, down_rows, preferred_element_type=jnp.float32
    )
    d_in_part = lax.dot_general(d_query_half, w_query, across, preferred_element_type=jnp.float32)
    d_in_part = d_in_part + lax.dot_general(
        d_key_half, w_key, across, preferred_element_type=jnp.float32
    )
    d_in_part = d_in_part + lax.dot_general(
        d_value_half, w_value, across, preferred_element_type=jnp.float32
    )
    d_in, g_query_gain, g_key_gain = lax.psum((d_in_part, g_query_part, g_key_part), "mp")
    d_in_norm, g_attn_gain = norm_back(inputs, scale_in, attn_gain, d_in)
    grad_tokens = d_hidden + d_in_norm
    totals = lax.psum(
        (g_query, g_key, g_value, g_out, g_query_gain, g_key_gain, g_attn_gain, g_ffn_gain), "dp"
    )
    weight_terms = jnp.concatenate(
        [
            jnp.concatenate(
                [
                    lax.dot_general(
                        normed_mid, d_gate, down_rows, preferred_element_type=jnp.float32
                    ),
                    lax.dot_general(
                        normed_mid, d_up, down_rows, preferred_element_type=jnp.float32
                    ),
                ],
                axis=1,
            ),
            lax.dot_general(grad_out, activated, down_rows, preferred_element_type=jnp.float32),
        ],
        axis=1,
    )
    mlp_grads = lax.psum_scatter(weight_terms, "dp", scatter_dimension=0, tiled=True)
    grad_w_gate = mlp_grads[:, :mid_width]
    grad_w_up = mlp_grads[:, mid_width : 2 * mid_width]
    grad_w_down = mlp_grads[:, 2 * mid_width :].T
    return (
        output,
        grad_tokens,
        totals[6],
        totals[0],
        totals[1],
        totals[2],
        totals[4],
        totals[5],
        totals[3],
        totals[7],
        grad_w_gate,
        grad_w_up,
        grad_w_down,
    )


def solution(mesh):
    placed = (
        P("dp", None),
        P("dp", None),
        P(),
        P(None, "mp"),
        P(None, "mp"),
        P(None, "mp"),
        P(),
        P(),
        P("mp", None),
        P(),
        P("dp", "mp"),
        P("dp", "mp"),
        P("mp", "dp"),
        P("dp", None),
    )
    return jax.shard_map(
        shards,
        mesh=mesh,
        in_specs=placed,
        out_specs=(
            P("dp", None),
            P("dp", None),
            P(),
            P(None, "mp"),
            P(None, "mp"),
            P(None, "mp"),
            P(),
            P(),
            P("mp", None),
            P(),
            P("dp", "mp"),
            P("dp", "mp"),
            P("mp", "dp"),
        ),
        check_vma=False,
    )
```

profile of v0, /device:TPU:0, one launch (start us, length us, event | category | flops | bytes accessed | tf_op | source)
XLA Modules:
  0.0 569.7 jit_solution(8897910424492054979)
XLA Ops:
  9.9 1.2 fusion.15
  11.2 1.5 convolution_convert_fusion.2
  12.7 1.5 multiply_reduce_fusion.6
  17.9 1.3 fusion.57
  22.9 35.4 %all-reduce.9.cloned.1.call-done = f32[256,1024]{1,0:T(8,128)} async-done(((f32[256,1024]{1,0:T(8,128)}), f32[256,1024]{1,0:T(8,128)}) %all-reduce.9.cloned.1.call-update) | async-done | bytes 1048592 | tf_op jit(solution)/shard_map/psum | solution.py:164
  58.3 1.4 multiply_reduce_fusion.2
  59.9 16.7 %all-gather.6.cloned.1.call-done = bf16[1024,1152]{1,0:T(8,128)(2,1)} async-done(((bf16[128,1152]{1,0:T(8,128)(2,1)}), bf16[1024,1152]{1,0:T(8,128)(2,1)}) %all-gather.6.cloned.1.call-update) | async-done | bytes 2359312 | tf_op jit(solution)/shard_map/all_gather | solution.py:169
  76.6 3.6 fusion.59
  80.3 49.0 %all-gather.4.cloned.1.call-done = bf16[1024,1152]{1,0:T(8,128)(2,1)} async-done(((bf16[128,1152]{1,0:T(8,128)(2,1)}), bf16[1024,1152]{1,0:T(8,128)(2,1)}) %all-gather.4.cloned.1.call-update) | async-done | bytes 2359312 | tf_op jit(solution)/shard_map/all_gather | solution.py:168
  129.3 3.6 fusion.58
  132.9 50.7 %all-gather.8.cloned.1.call-done = bf16[1152,1024]{1,0:T(8,128)(2,1)} async-done(((bf16[1152,128]{1,0:T(8,128)(2,1)}), bf16[1152,1024]{1,0:T(8,128)(2,1)}) %all-gather.8.cloned.1.call-update) | async-done | bytes 2359312 | tf_op jit(solution)/shard_map/all_gather | solution.py:178
  183.6 4.5 multiply_convert_fusion
  189.1 1.1 copy-done.5
  190.2 1.9 convolution_add_fusion.1
  192.4 4.2 convolution_bitcast_fusion
  196.6 1.8 fusion.60
  198.4 3.1 fusion.65
  201.5 25.0 %all-reduce.11.cloned.1.call-done = f32[256,1024]{1,0:T(8,128)} async-done(((f32[256,1024]{1,0:T(8,128)}), f32[256,1024]{1,0:T(8,128)}) %all-reduce.11.cloned.1.call-update) | async-done | bytes 1048592 | tf_op jit(solution)/shard_map/psum | solution.py:197
  226.5 2.2 multiply_reduce_fusion
  228.7 1.1 subtract_add_fusion
  229.8 1.0 copy-done.3
  231.2 1.6 fusion.9
  232.8 1.7 fusion.6
  234.8 1.0 fusion.40
  237.5 1.3 fusion
  238.9 2.0 fusion.64
  240.8 9.5 %pad_maximum_fusion = f32[1024,3456]{1,0:T(8,128)} fusion(f32[1024,1152]{1,0:T(8,128)} %convolution_bitcast_fusion, f32[1024,1152]{1,0:T(8,128)} %fusion.65, f32[1024,1152]{1,0:T(8,128)S(1)} %fusion.64), kind=kLoop, calls=%fused_computation | loop fusion | flops 7077888 | bytes 28311552 | tf_op jit(solution)/shard_map/concatenate | solution.py:239
  251.2 1.3 fusion.47
  252.4 1.2 fusion.45
  253.7 1.5 fusion.49
  255.1 1.3 fusion.34
  257.6 1.1 rsqrt.45
  259.7 0.9 reshape.229
  261.6 1.1 copy.109
  262.7 1.9 copy.110
  264.7 1.2 fusion.32
  265.9 1.6 fusion.23
  267.5 6.5 %all-reduce.2 = (f32[64]{0:T(128)S(1)}, f32[64]{0:T(128)S(1)}) all-reduce(f32[64]{0:T(128)S(1)} %fusion.23, f32[64]{0:T(128)S(1)} %fusion.32), channel_id=1, replica_groups=mesh['dp'=8,'mp'=4] {'mp'}, use_global_device_ids=true, to_apply=%region_22.23 | all-reduce | flops 128 | bytes 1024 | tf_op jit(solution)/shard_map/psum | solution.py:233
  273.9 17.1 %all-reduce.15.cloned.1.call-done = (f32[256,1024]{1,0:T(8,128)}, f32[256,1024]{1,0:T(8,128)}) async-done(((f32[256,1024]{1,0:T(8,128)}, f32[256,1024]{1,0:T(8,128)}), (f32[256,1024]{1,0:T(8,128)}, f32[256,1024]{1,0:T(8,128)})) %all-reduce.15.cloned.1.call-update) | async-done | bytes 2097168 | tf_op jit(solution)/shard_map/psum | solution.py:181
  291.0 1.6 fusion.18
  292.6 24.3 %all-reduce = (f32[1024]{0:T(1024)}, f32[64]{0:T(128)}, f32[64]{0:T(128)}, f32[1024]{0:T(1024)}) all-reduce(f32[1024]{0:T(1024)S(1)} %get-tuple-element.80, f32[64]{0:T(128)S(1)} %get-tuple-element.90, f32[64]{0:T(128)S(1)} %get-tuple-element.91, f32[1024]{0:T(1024)S(1)} %copy-done.47), channel_id=1, replica_groups=mesh['dp'=8,'mp'=4] {'dp'}, use_global_device_ids=true, to_apply=%region_17.18 | all-reduce | flops 2176 | bytes 17408 | tf_op jit(solution)/shard_map/psum | solution.py:236
  316.9 3.0 fusion.14
  319.9 227.3 %reduce-scatter.2.cloned.1.call-done = f32[128,3456]{1,0:T(8,128)} async-done(((f32[1024,3456]{1,0:T(8,128)}), f32[128,3456]{1,0:T(8,128)}) %reduce-scatter.2.cloned.1.call-update) | async-done | bytes 1769488 | tf_op jit(solution)/shard_map/reduce_scatter | solution.py:256
  547.2 2.5 slice_bitcast_fusion
  549.7 1.0 copy.118
  550.8 6.5 %all-reduce.13.cloned.1.call-done = (f32[1024,256]{1,0:T(8,128)}, f32[1024,128]{1,0:T(8,128)}, f32[1024,128]{1,0:T(8,128)}, f32[256,1024]{1,0:T(8,128)}) async-done(((f32[1024,256]{1,0:T(8,128)}, f32[1024,128]{1,0:T(8,128)}, f32[1024,128]{1,0:T(8,128)}, f32[256,1024]{1,0:T(8,128)}), (f32[1024,256]{1,0:T(8,128)}, f32[1024,128]{1,0:T(8,128)}, f32[1024,128]{1,0:T(8,128)}, ...) | async-done | bytes 3145744 | tf_op jit(solution)/shard_map/psum | solution.py:236
  557.3 2.4 copy.137
  561.3 1.0 copy.140
  (179 shorter events, 18.1 us)
Async XLA Ops:
  8.0 9.9 %copy-start = (bf16[256,1024]{1,0:T(8,128)(2,1)S(1)}, bf16[256,1024]{1,0:T(8,128)(2,1)}, u32[]{:S(2)}) copy-start(bf16[256,1024]{1,0:T(8,128)(2,1)} %param.22) | copy-start | bytes 1572868
  8.0 6.3 %copy-start.2 = (bf16[256,1024]{1,0:T(8,128)(2,1)S(1)}, bf16[256,1024]{1,0:T(8,128)(2,1)}, u32[]{:S(2)}) copy-start(bf16[256,1024]{1,0:T(8,128)(2,1)} %param.14) | copy-start | bytes 1572868
  8.0 6.3 %copy-start.41 = (f32[1024]{0:T(1024)S(1)}, f32[1024]{0:T(1024)}, u32[]{:S(2)}) copy-start(f32[1024]{0:T(1024)} %param.16) | copy-start | bytes 12292
  8.1 6.3 %copy-start.29 = (bf16[1024,256]{1,0:T(8,128)(2,1)S(1)}, bf16[1024,256]{1,0:T(8,128)(2,1)}, u32[]{:S(2)}) copy-start(bf16[1024,256]{1,0:T(8,128)(2,1)} %param.17) | copy-start | bytes 1572868
  8.1 7.0 %copy-start.53 = (f32[64]{0:T(128)S(1)}, f32[64]{0:T(128)}, u32[]{:S(2)}) copy-start(f32[64]{0:T(128)} %param.21) | copy-start | bytes 772
  8.1 50.2 %all-reduce.9.cloned.1.call-start = ((), (), s32[]{:S(2)}) async-start(), calls=%async_computation.1 | async-start | bytes 2097152 | tf_op jit(solution)/shard_map/psum | solution.py:164
  9.9 5.7 %copy-start.42 = (pred[256,256]{0,1:T(8,128)(4,1)}, pred[256,256]{0,1:T(8,128)(4,1)S(1)}, u32[]{:S(2)}) copy-start(pred[256,256]{0,1:T(8,128)(4,1)S(1)} %compare_and_fusion) | copy-start | bytes 196612
  11.2 4.0 copy-start.49
  12.7 3.8 copy-start.56
  14.3 2.2 copy-start.45
  19.2 40.5 %copy-start.44 = (f32[1024]{0:T(1024)S(1)}, f32[1024]{0:T(1024)}, u32[]{:S(2)}) copy-start(f32[1024]{0:T(1024)} %param.23) | copy-start | bytes 12292
  19.3 57.4 %all-gather.6.cloned.1.call-start = ((), (), s32[]{:S(2)}) async-start(), calls=%async_computation.3 | async-start | bytes 2654208 | tf_op jit(solution)/shard_map/all_gather | solution.py:169
  19.8 109.4 %all-gather.4.cloned.1.call-start = ((), (), s32[]{:S(2)}) async-start(), calls=%async_computation.2 | async-start | bytes 2654208 | tf_op jit(solution)/shard_map/all_gather | solution.py:168
  20.4 163.2 %all-gather.8.cloned.1.call-start = ((), (), s32[]{:S(2)}) async-start(), calls=%async_computation.4 | async-start | bytes 2654208 | tf_op jit(solution)/shard_map/all_gather | solution.py:178
  21.0 205.5 %all-reduce.11.cloned.1.call-start = ((), (), s32[]{:S(2)}) async-start(), calls=%async_computation.5 | async-start | bytes 2097152 | tf_op jit(solution)/shard_map/psum | solution.py:197
  59.7 16.9 %copy-start.48 = (f32[256]{0:T(256)}, f32[256]{0:T(256)S(1)}, u32[]{:S(2)}) copy-start(f32[256]{0:T(256)S(1)} %add_rsqrt_fusion.2) | copy-start | bytes 3076
  80.2 103.3 %copy-start.13 = (bf16[256,1024]{1,0:T(8,128)(2,1)S(1)}, bf16[256,1024]{1,0:T(8,128)(2,1)}, u32[]{:S(2)}) copy-start(bf16[256,1024]{1,0:T(8,128)(2,1)} %param.27) | copy-start | bytes 1572868
  183.6 4.5 copy-start.6
  188.1 2.1 copy-start.5
  192.1 98.9 %all-reduce.15.cloned.1.call-start = ((), (), s32[]{:S(2)}) async-start(), calls=%async_computation.8 | async-start | bytes 4194304 | tf_op jit(solution)/shard_map/psum | solution.py:181
  192.3 4.3 copy-start.8
  192.3 4.2 copy-start.12
  196.6 1.8 copy-start.10
  226.5 2.2 copy-start.7
  228.7 2.0 copy-start.15
  230.7 2.0 copy-start.43
  230.7 2.0 copy-start.52
  230.7 2.0 copy-start.57
  230.7 3.7 copy-start.32
  230.7 3.7 copy-start.34
  231.1 4.7 copy-start.22
  231.2 4.7 copy-start.24
  232.7 3.5 copy-start.37
  232.7 3.2 copy-start.54
  232.8 3.3 copy-start.50
  234.8 1.8 copy-start.46
  234.8 1.8 copy-start.55
  234.8 1.9 copy-start.36
  238.8 308.4 %reduce-scatter.2.cloned.1.call-start = ((), (), s32[]{:S(2)}) async-start(), calls=%async_computation.6 | async-start | bytes 15925248 | tf_op jit(solution)/shard_map/reduce_scatter | solution.py:256
  250.3 2.1 copy-start.38
  250.4 4.8 copy-start.4
  250.4 4.8 copy-start.16
  250.4 306.9 %all-reduce.13.cloned.1.call-start = ((), (), s32[]{:S(2)}) async-start(), calls=%async_computation.7 | async-start | bytes 6291456 | tf_op jit(solution)/shard_map/psum | solution.py:236
  262.7 29.8 %copy-start.47 = (f32[1024]{0:T(1024)S(1)}, f32[1024]{0:T(1024)}, u32[]{:S(2)}) copy-start(f32[1024]{0:T(1024)} %get-tuple-element.78) | copy-start | bytes 12292
  557.3 2.4 copy-start.28
  557.3 3.2 copy-start.27
  557.3 4.0 copy-start.20
  557.3 5.0 copy-start.1
  (18 other events, 18.7 us)
Sparse Core Ops, SparseCore 0:
  19.4 38.8 all-reduce.8
  192.2 34.2 all-reduce.10
  238.9 52.0 all-reduce.14
  295.8 261.4 all-reduce.12
Sparse Core Ops, SparseCore 1:
  22.2 54.4 all-gather.5
  78.9 50.3 all-gather.3
  131.4 52.2 all-gather.7
  250.4 296.7 reduce-scatter.1
where the time goes:
time: 571 us; the launch traced here: 570 us
  waiting for transfers between devices  429 us (75%)
  matrix products  43.1 us (8%)
  blocking collectives  30.8 us (5%)
  other arithmetic  26.4 us (5%)
  local copies, waits for them, and re-layouts  23.1 us (4%)
  between operations  16.3 us (3%)
    reduce_scatter x1, waiting for transfers between devices, shards(): lax.psum_scatter(weight_terms, 'dp', scatter_dimension=0, tiled=True)  227 us
    all_gather x1, waiting for transfers between devices, shards(): lax.all_gather(w_down, 'dp', axis=1, tiled=True)  50.7 us
    all_gather x1, waiting for transfers between devices, shards(): lax.all_gather(w_gate, 'dp', axis=0, tiled=True)  49 us
    psum x1, waiting for transfers between devices, shards(): hidden = inputs + lax.psum(head_part, 'mp')  35.4 us
    psum x1, waiting for transfers between devices, shards(): d_mid = lax.psum(d_mid_part, 'mp')  25 us
    psum x1, blocking collectives, shards(): lax.psum((g_query, g_key, g_value, g_out, g_query_gain, g_key_gain, g_att...  24.3 us
    psum x1, waiting for transfers between devices, shards(): output = (hidden + lax.psum(ffn_part, 'mp')).astype(jnp.bfloat16)  17.1 us
    all_gather x1, waiting for transfers between devices, shards(): lax.all_gather(w_up, 'dp', axis=0, tiled=True)  16.7 us
  transfers between devices with their start and end apart: 8, of which 8 were waited for; matrix products, arithmetic and copies ran while one was open for 10% of the time, Pallas kernels for 0%

commit v1 on v0

--- a/solution.py
+++ b/solution.py
@@ -1,8 +1,11 @@
+import functools
 import math
 
 import jax
 import jax.numpy as jnp
 from jax import lax
+from jax.experimental import pallas as pl
+from jax.experimental.pallas import tpu as pltpu
 from jax.sharding import PartitionSpec as P
 
 HEAD_DIM = 64
@@ -116,7 +119,403 @@
     return (d_query_rot, d_key_rot, d_value)
 
 
+RING_LIMIT = 16
+
+
+def ring_order(count):
+    return tuple(range(0, count, 2)) + tuple(range(count - 1, 0, -2))
+
+
+def ring_moves(count):
+    order = ring_order(count)
+    ahead = [(order[i], order[(i + 1) % count]) for i in range(count)]
+    back = [(order[(i + 1) % count], order[i]) for i in range(count)]
+    return ahead, back
+
+
+def ring_place(count):
+    order = ring_order(count)
+    place = [0] * count
+    for spot, owner in enumerate(order):
+        place[owner] = spot
+    me = jnp.array(place, dtype=jnp.int32)[lax.axis_index("dp")]
+    table = jnp.array(order, dtype=jnp.int32)
+    return lambda step: table[(me + step + 2 * count) % count]
+
+
+class Gather:
+    def __init__(self, block, count):
+        self.count, self.block = count, block
+        self.ring = count >= 4 and count % 2 == 0 and count <= RING_LIMIT
+        self.left = self.right = block
+        self.done = 0
+        if self.ring:
+            self.owner = ring_place(count)
+            self.moves = ring_moves(count)
+            self.whole = None
+
+    def put(self, piece, who, shift=0):
+        start = who * self.block.shape[0] + shift
+        self.whole = lax.dynamic_update_slice_in_dim(self.whole, piece, start, 0)
+
+    def step(self):
+        if not self.ring or self.done >= self.count // 2:
+            return
+        self.done += 1
+        ahead, back = self.moves
+        half = self.block.shape[0] // 2
+        if self.done < self.count // 2:
+            self.left = lax.ppermute(self.left, "dp", ahead)
+            self.right = lax.ppermute(self.right, "dp", back)
+            if self.whole is None:
+                zero, self.left, self.right = lax.optimization_barrier(
+                    (jnp.zeros((), self.block.dtype), self.left, self.right)
+                )
+                self.whole = jnp.broadcast_to(
+                    zero, (self.count * self.block.shape[0],) + self.block.shape[1:]
+                )
+                self.put(self.block, self.owner(0))
+            self.put(self.left, self.owner(-self.done))
+            self.put(self.right, self.owner(self.done))
+        else:
+            far = self.owner(self.done)
+            self.put(lax.ppermute(self.left[:half], "dp", ahead), far)
+            self.put(lax.ppermute(self.right[half:], "dp", back), far, half)
+
+    def tie(self, value):
+        if not self.ring:
+            return value
+        value, self.left, self.right = lax.optimization_barrier((value, self.left, self.right))
+        self.step()
+        return value
+
+    def result(self):
+        if self.count == 1:
+            return self.block
+        if not self.ring:
+            return lax.all_gather(self.block, "dp", axis=0, tiled=True)
+        while self.done < self.count // 2:
+            self.step()
+        return self.whole
+
+
+class Scatter:
+    def __init__(self, terms, count):
+        self.count, self.terms = count, terms
+        self.ring = count >= 4 and count % 2 == 0 and count <= RING_LIMIT
+        if not self.ring:
+            return
+        self.rows = terms.shape[0] // count
+        self.owner = ring_place(count)
+        self.moves = ring_moves(count)
+        self.left = count // 2
+        half = self.rows // 2
+        self.cw = self.term(self.left, 0, half)
+        self.ccw = self.term(self.left, half, half)
+        self.send()
+
+    def term(self, step, start=0, size=None):
+        return lax.dynamic_slice_in_dim(
+            self.terms, self.owner(step) * self.rows + start, size or self.rows, 0
+        )
+
+    def plus(self, one, two):
+        return (one.astype(jnp.float32) + two.astype(jnp.float32)).astype(self.terms.dtype)
+
+    def send(self):
+        self.cw = lax.ppermute(self.cw, "dp", self.moves[0])
+        self.ccw = lax.ppermute(self.ccw, "dp", self.moves[1])
+        self.left -= 1
+
+    def step(self):
+        if not self.ring or self.left == 0:
+            return
+        step, half = self.left, self.rows // 2
+        if step == self.count // 2 - 1:
+            self.cw = jnp.concatenate(
+                [self.plus(self.term(step, 0, half), self.cw), self.term(step, half, half)], axis=0
+            )
+            self.ccw = jnp.concatenate(
+                [self.term(-step, 0, half), self.plus(self.term(-step, half, half), self.ccw)],
+                axis=0,
+            )
+        else:
+            self.cw = self.plus(self.term(step), self.cw)
+            self.ccw = self.plus(self.term(-step), self.ccw)
+        self.send()
+
+    def finished(self, value):
+        if not self.ring:
+            return value
+        while self.left:
+            self.step()
+        value, self.cw, self.ccw = lax.optimization_barrier((value, self.cw, self.ccw))
+        return value
+
+    def tie(self, value):
+        if not self.ring or self.left == 0:
+            return value
+        value, self.cw, self.ccw = lax.optimization_barrier((value, self.cw, self.ccw))
+        self.step()
+        return value
+
+    def result(self):
+        if self.count == 1:
+            return self.terms.astype(jnp.float32)
+        if not self.ring:
+            total = lax.psum_scatter(self.terms, "dp", scatter_dimension=0, tiled=True)
+            return total.astype(jnp.float32)
+        while self.left:
+            self.step()
+        own = self.term(0).astype(jnp.float32)
+        return own + self.cw.astype(jnp.float32) + self.ccw.astype(jnp.float32)
+
+
+def sum_all(vector, sizes):
+    for name, count in sizes:
+        if count & (count - 1) or count > RING_LIMIT:
+            vector = lax.psum(vector, name)
+            continue
+        reach = 1
+        while reach < count:
+            pairs = [(i, i ^ reach) for i in range(count)]
+            vector = vector + lax.ppermute(vector, name, pairs)
+            reach *= 2
+    return vector
+
+
+def sum_heads(part, count, tie=lambda value: value):
+    if count != 4:
+        return lax.psum(part, "mp")
+    near = [(i, i ^ 1) for i in range(count)]
+    across = [(i, i ^ 2) for i in range(count)]
+    half = part.shape[0] // 2
+    bit = lax.axis_index("mp") % 2
+    kept = lax.dynamic_slice_in_dim(part, bit * half, half, 0)
+    given = lax.dynamic_slice_in_dim(part, (1 - bit) * half, half, 0).astype(jnp.bfloat16)
+    mine = kept + lax.ppermute(given, "mp", near).astype(jnp.float32)
+    mine = tie(lax.reduce_precision(mine, 8, 7))
+    other = lax.ppermute(mine.astype(jnp.bfloat16), "mp", across)
+    mine = mine + other.astype(jnp.float32)
+    other = lax.ppermute(mine, "mp", near)
+    return jnp.where(
+        bit == 0,
+        jnp.concatenate([mine, other], axis=0),
+        jnp.concatenate([other, mine], axis=0),
+    )
+
+
+MESH_ID = pl.DeviceIdType.MESH
+
+
+def finish_kernel(
+    count,
+    terms,
+    part,
+    vector,
+    grads,
+    total,
+    gains,
+    cw_in,
+    ccw_in,
+    cw_out,
+    ccw_out,
+    near_out,
+    near_in,
+    far_out,
+    far_in,
+    vec_out,
+    vec_in,
+    ring_send,
+    ring_recv,
+    pair_send,
+    pair_recv,
+    vec_send,
+    vec_recv,
+):
+    dp, mp = lax.axis_index("dp"), lax.axis_index("mp")
+    rows = terms.shape[0] // count
+    half = rows // 2
+    far = count // 2
+
+    def owner(spot):
+        spot = lax.rem(spot + 2 * count, count)
+        low = 1 - spot // far
+        return low * 2 * spot + (1 - low) * (2 * (count - spot) - 1)
+
+    odd = lax.rem(dp, 2)
+    place = (1 - odd) * (dp // 2) + odd * (count - (dp + 1) // 2)
+    ahead, behind = (owner(place + 1), mp), (owner(place - 1), mp)
+
+    def pair(value, reach):
+        return value + reach * (1 - 2 * lax.rem(value // reach, 2))
+
+    partners = [(dp, pair(mp, 1)), (dp, pair(mp, 2))]
+    reach = 1
+    while reach < count:
+        partners.append((pair(dp, reach), mp))
+        reach *= 2
+
+    barrier = pltpu.get_barrier_semaphore()
+    for target in [ahead, behind] + partners:
+        pl.semaphore_signal(barrier, inc=1, device_id=target, device_id_type=MESH_ID)
+    pl.semaphore_wait(barrier, 2 + len(partners))
+
+    def send(source, dest, sems, target):
+        copy = pltpu.make_async_remote_copy(
+            src_ref=source,
+            dst_ref=dest,
+            send_sem=sems[0],
+            recv_sem=sems[1],
+            device_id=target,
+            device_id_type=MESH_ID,
+        )
+        copy.start()
+        return copy
+
+    def rows_of(spot, start=0, size=None):
+        return pl.ds(pl.multiple_of(owner(place + spot) * rows + start, 16), size or rows)
+
+    def term(spot, start=0, size=None):
+        return terms[rows_of(spot, start, size), :].astype(jnp.float32)
+
+    def ring_sems(way, turn):
+        return ring_send.at[way, turn], ring_recv.at[way, turn]
+
+    cw = send(
+        terms.at[rows_of(far, 0, half), :], cw_in.at[0, pl.ds(0, half)], ring_sems(0, 0), ahead
+    )
+    ccw = send(
+        terms.at[rows_of(-far, half, half), :],
+        ccw_in.at[0, pl.ds(half, half)],
+        ring_sems(1, 0),
+        behind,
+    )
+
+    bit = lax.rem(mp, 2)
+    middle = part.shape[0] // 2
+    kept = pl.ds(pl.multiple_of(bit * middle, 16), middle)
+    given = pl.ds(pl.multiple_of((1 - bit) * middle, 16), middle)
+    near_out[...] = part[given, :].astype(jnp.bfloat16)
+    pairs = [send(near_out, near_in, (pair_send.at[0], pair_recv.at[0]), partners[0])]
+
+    vec_out[0] = vector[...]
+    vecs = [send(vec_out.at[0], vec_in.at[0], (vec_send.at[0], vec_recv.at[0]), partners[0])]
+
+    def vector_turn():
+        turn = len(vecs) - 1
+        if turn >= len(partners):
+            return
+        vecs[turn].wait()
+        both = vec_out[turn] + vec_in[turn]
+        if turn + 1 == len(partners):
+            gains[...] = both
+            vecs.append(None)
+            return
+        vec_out[turn + 1] = both
+        sems = (vec_send.at[turn + 1], vec_recv.at[turn + 1])
+        vecs.append(send(vec_out.at[turn + 1], vec_in.at[turn + 1], sems, partners[turn + 1]))
+
+    def pair_turn():
+        turn = len(pairs)
+        if turn == 1:
+            pairs[0].wait()
+            far_out[...] = (part[kept, :] + near_in[...].astype(jnp.float32)).astype(jnp.bfloat16)
+            pairs.append(send(far_out, far_in, (pair_send.at[1], pair_recv.at[1]), partners[1]))
+        elif turn == 2:
+            pairs[1].wait()
+            total[kept, :] = far_out[...].astype(jnp.float32) + far_in[...].astype(jnp.float32)
+            view = total.at[kept, :]
+            pairs.append(send(view, view, (pair_send.at[2], pair_recv.at[2]), partners[0]))
+        elif turn == 3:
+            pairs[2].wait()
+            pairs.append(None)
+
+    for turn in range(1, far):
+        spot = far - turn
+        cw.wait()
+        if turn == 1:
+            low, high = pl.ds(0, half), pl.ds(half, half)
+            cw_out[0, low] = (term(spot, 0, half) + cw_in[0, low].astype(jnp.float32)).astype(
+                jnp.bfloat16
+            )
+            cw_out[0, high] = terms[rows_of(spot, half, half), :]
+        else:
+            cw_out[turn - 1] = (term(spot) + cw_in[turn - 1].astype(jnp.float32)).astype(
+                jnp.bfloat16
+            )
+        cw = send(cw_out.at[turn - 1], cw_in.at[turn], ring_sems(0, turn), ahead)
+        ccw.wait()
+        if turn == 1:
+            ccw_out[0, high] = (
+                term(-spot, half, half) + ccw_in[0, high].astype(jnp.float32)
+            ).astype(jnp.bfloat16)
+            ccw_out[0, low] = terms[rows_of(-spot, 0, half), :]
+        else:
+            ccw_out[turn - 1] = (term(-spot) + ccw_in[turn - 1].astype(jnp.float32)).astype(
+                jnp.bfloat16
+            )
+        ccw = send(ccw_out.at[turn - 1], ccw_in.at[turn], ring_sems(1, turn), behind)
+        pair_turn()
+        vector_turn()
+    cw.wait()
+    ccw.wait()
+    own = term(0) + cw_in[far - 1].astype(jnp.float32) + ccw_in[far - 1].astype(jnp.float32)
+    grads[rows_of(0), :] = own.astype(jnp.bfloat16)
+
+    for turn in range(1, far + 1):
+        size = rows if turn < far else half
+        shift = 0 if turn < far else half
+        one = grads.at[rows_of(1 - turn, 0, size), :]
+        two = grads.at[rows_of(turn - 1, shift, size), :]
+        cw = send(one, one, ring_sems(0, far + turn - 1), ahead)
+        ccw = send(two, two, ring_sems(1, far + turn - 1), behind)
+        pair_turn()
+        vector_turn()
+        cw.wait()
+        ccw.wait()
+    while len(pairs) < 4:
+        pair_turn()
+    while len(vecs) <= len(partners):
+        vector_turn()
+
+
+def finish(terms, part, vector, dp_count):
+    rows, columns = terms.shape[0] // dp_count, terms.shape[1]
+    far, steps = dp_count // 2, 2 + dp_count.bit_length() - 1
+    lanes = 128
+    tall = -(-vector.shape[0] // (8 * lanes)) * 8
+    padded = jnp.pad(vector, (0, tall * lanes - vector.shape[0])).reshape(tall, lanes)
+    middle = (part.shape[0] // 2, part.shape[1])
+    ring_slots = pltpu.VMEM((far, rows, columns), jnp.bfloat16)
+    half_slot = pltpu.VMEM(middle, jnp.bfloat16)
+    vec_slots = pltpu.VMEM((steps, tall, lanes), jnp.float32)
+    vmem = pl.BlockSpec(memory_space=pltpu.VMEM)
+    grads, total, gains = pl.pallas_call(
+        functools.partial(finish_kernel, dp_count),
+        out_shape=(
+            jax.ShapeDtypeStruct(terms.shape, jnp.bfloat16),
+            jax.ShapeDtypeStruct(part.shape, jnp.float32),
+            jax.ShapeDtypeStruct(padded.shape, jnp.float32),
+        ),
+        in_specs=[vmem] * 3,
+        out_specs=(vmem,) * 3,
+        scratch_shapes=[ring_slots] * 4
+        + [half_slot] * 4
+        + [vec_slots] * 2
+        + [pltpu.SemaphoreType.DMA((2, 2 * far))] * 2
+        + [pltpu.SemaphoreType.DMA((3,))] * 2
+        + [pltpu.SemaphoreType.DMA((steps,))] * 2,
+        compiler_params=pltpu.CompilerParams(
+            collective_id=0, has_side_effects=True, vmem_limit_bytes=24 * 1024 * 1024
+        ),
+    )(terms, part, padded)
+    return grads, total, gains.reshape(-1)[: vector.shape[0]]
+
+
 def shards(
+    dp_count,
+    mp_count,
     tokens,
     segment_ids,
     attn_gain,
@@ -132,21 +531,26 @@
     w_down,
     grad_out,
 ):
-    token_count = tokens.shape[0]
-    mid_width = w_gate.shape[1]
+    token_count, width = tokens.shape
     across = (((1,), (1,)), ((), ()))
     down_rows = (((0,), (0,)), ((), ()))
+    mid_width = w_gate.shape[1]
+    block = jnp.concatenate([w_gate, w_up, w_down.T], axis=1)
+    tokens, block = lax.optimization_barrier((tokens, block))
+    ring = Gather(block, dp_count)
+    ring.step()
+    w_heads = jnp.concatenate([w_query, w_key, w_value], axis=1)
+    query_width, key_width = w_query.shape[1], w_key.shape[1]
     inputs = tokens.astype(jnp.float32)
     scale_in = rms_scale(inputs)
     normed_in = (inputs * scale_in * attn_gain).astype(jnp.bfloat16)
-    query_proj = jnp.dot(normed_in, w_query, preferred_element_type=jnp.float32).reshape(
+    heads_proj = jnp.dot(normed_in, w_heads, preferred_element_type=jnp.float32)
+    query_proj = heads_proj[:, :query_width].reshape(token_count, -1, HEAD_DIM)
+    key_proj = heads_proj[:, query_width : query_width + key_width].reshape(
         token_count, -1, HEAD_DIM
     )
-    key_proj = jnp.dot(normed_in, w_key, preferred_element_type=jnp.float32).reshape(
-        token_count, -1, HEAD_DIM
-    )
     value_half = (
-        jnp.dot(normed_in, w_value, preferred_element_type=jnp.float32)
+        heads_proj[:, query_width + key_width :]
         .astype(jnp.bfloat16)
         .reshape(token_count, -1, HEAD_DIM)
     )
@@ -159,54 +563,57 @@
     )
     key_rot = rotate(key_proj * key_scale * key_gain, cosine, sine_table).astype(jnp.bfloat16)
     attended, logsum = attention_forward(query_rot, key_rot, value_half, allowed)
-    attn_flat = attended.reshape(token_count, -1)
+    attn_flat = ring.tie(attended.reshape(token_count, -1))
     head_part = jnp.dot(attn_flat, w_out, preferred_element_type=jnp.float32)
-    hidden = inputs + lax.psum(head_part, "mp")
+    hidden = inputs + sum_heads(head_part, mp_count)
     scale_mid = rms_scale(hidden)
+    weights = ring.result()
     normed_mid = (hidden * scale_mid * ffn_gain).astype(jnp.bfloat16)
-    pieces = (
-        lax.all_gather(w_gate, "dp", axis=0, tiled=True),
-        lax.all_gather(w_up, "dp", axis=0, tiled=True),
-    )
-    columns = normed_mid
-    gate_proj = jnp.dot(columns, pieces[0], preferred_element_type=jnp.float32)
-    up_proj = jnp.dot(columns, pieces[1], preferred_element_type=jnp.float32)
+    both = jnp.dot(normed_mid, weights[:, : 2 * mid_width], preferred_element_type=jnp.float32)
+    gate_proj = both[:, :mid_width]
+    up_proj = both[:, mid_width:]
     sig_gate = jax.nn.sigmoid(gate_proj)
     activated = (gate_proj * sig_gate * up_proj).astype(jnp.bfloat16)
-    ffn_part = jnp.dot(
-        activated,
-        lax.all_gather(w_down, "dp", axis=1, tiled=True),
-        preferred_element_type=jnp.float32,
-    )
-    output = (hidden + lax.psum(ffn_part, "mp")).astype(jnp.bfloat16)
-    columns = grad_out
-    d_act = lax.dot_general(
-        columns,
-        lax.all_gather(w_down, "dp", axis=1, tiled=True),
-        across,
-        preferred_element_type=jnp.float32,
-    )
+    w_back = weights[:, 2 * mid_width :]
+    d_act = jnp.dot(grad_out, w_back, preferred_element_type=jnp.float32)
     d_up = (d_act * gate_proj * sig_gate).astype(jnp.bfloat16)
     d_gate = (d_act * up_proj * sig_gate * (1.0 + gate_proj * (1.0 - sig_gate))).astype(
         jnp.bfloat16
     )
-    pieces = lax.all_gather((w_gate, w_up), "dp", axis=0, tiled=True)
+    d_both = jnp.concatenate([d_gate, d_up], axis=1)
+    mlp_terms = jnp.concatenate(
+        [
+            lax.dot_general(
+                normed_mid, d_both, down_rows, preferred_element_type=jnp.float32
+            ).astype(jnp.bfloat16),
+            lax.dot_general(
+                grad_out, activated, down_rows, preferred_element_type=jnp.float32
+            ).astype(jnp.bfloat16),
+        ],
+        axis=1,
+    )
     d_mid_part = lax.dot_general(
-        d_gate, pieces[0], across, preferred_element_type=jnp.float32
-    ) + lax.dot_general(d_up, pieces[1], across, preferred_element_type=jnp.float32)
-    d_mid = lax.psum(d_mid_part, "mp")
-    d_hidden_norm, g_ffn_gain = norm_back(hidden, scale_mid, ffn_gain, d_mid)
+        d_both, weights[:, : 2 * mid_width], across, preferred_element_type=jnp.float32
+    )
+    mlp_sum = Scatter(mlp_terms, dp_count)
+    d_mid = sum_heads(d_mid_part, mp_count, mlp_sum.tie)
+    ffn_part = lax.dot_general(activated, w_back, across, preferred_element_type=jnp.float32)
+    output = (hidden + sum_heads(ffn_part, mp_count)).astype(jnp.bfloat16)
+    g_ffn_gain = jnp.sum(d_mid_part * hidden * scale_mid, axis=0)
+    d_hidden_norm, _ = norm_back(hidden, scale_mid, ffn_gain, d_mid)
     d_hidden = grad_out.astype(jnp.float32) + d_hidden_norm
     d_hidden_half = d_hidden.astype(jnp.bfloat16)
-    g_out = lax.dot_general(attn_flat, d_hidden_half, down_rows, preferred_element_type=jnp.float32)
+    g_out = lax.dot_general(d_hidden_half, attn_flat, down_rows, preferred_element_type=jnp.float32)
     d_attended = (
         lax.dot_general(d_hidden_half, w_out, across, preferred_element_type=jnp.float32)
         .astype(jnp.bfloat16)
         .reshape(token_count, -1, HEAD_DIM)
     )
+    d_attended = mlp_sum.tie(d_attended)
     d_query_rot, d_key_rot, d_value = attention_backward(
         query_rot, key_rot, value_half, allowed, attended, logsum, d_attended
     )
+    d_query_rot = mlp_sum.tie(d_query_rot)
     d_query, g_query_part = norm_back(
         query_proj, query_scale, query_gain, rotate_back(d_query_rot, cosine, sine_table)
     )
@@ -216,61 +623,42 @@
     d_query_half = d_query.astype(jnp.bfloat16).reshape(token_count, -1)
     d_key_half = d_key.astype(jnp.bfloat16).reshape(token_count, -1)
     d_value_half = d_value.reshape(token_count, -1)
-    g_query = lax.dot_general(
-        normed_in, d_query_half, down_rows, preferred_element_type=jnp.float32
-    )
-    g_key = lax.dot_general(normed_in, d_key_half, down_rows, preferred_element_type=jnp.float32)
-    g_value = lax.dot_general(
-        normed_in, d_value_half, down_rows, preferred_element_type=jnp.float32
-    )
-    d_in_part = lax.dot_general(d_query_half, w_query, across, preferred_element_type=jnp.float32)
-    d_in_part = d_in_part + lax.dot_general(
-        d_key_half, w_key, across, preferred_element_type=jnp.float32
-    )
-    d_in_part = d_in_part + lax.dot_general(
-        d_value_half, w_value, across, preferred_element_type=jnp.float32
-    )
-    d_in, g_query_gain, g_key_gain = lax.psum((d_in_part, g_query_part, g_key_part), "mp")
-    d_in_norm, g_attn_gain = norm_back(inputs, scale_in, attn_gain, d_in)
+    d_heads = jnp.concatenate([d_query_half, d_key_half, d_value_half], axis=1)
+    g_heads = lax.dot_general(normed_in, d_heads, down_rows, preferred_element_type=jnp.float32)
+    d_in_part = lax.dot_general(d_heads, w_heads, across, preferred_element_type=jnp.float32)
+    g_attn_gain = jnp.sum(d_in_part * inputs * scale_in, axis=0)
+    vector = jnp.concatenate([g_attn_gain, g_ffn_gain, g_query_part, g_key_part])
+    attn_terms = jnp.concatenate(
+        [g_heads.astype(jnp.bfloat16), g_out.astype(jnp.bfloat16)], axis=1
+    )
+    attn_terms = mlp_sum.finished(attn_terms)
+    if dp_count in (4, 8, 16) and mp_count == 4:
+        attn_grads, d_in, gains = finish(attn_terms, d_in_part, vector, dp_count)
+    else:
+        attn_own = Scatter(attn_terms, dp_count).result().astype(jnp.bfloat16)
+        attn_grads = Gather(attn_own, dp_count).result()
+        gains = sum_all(vector, (("mp", mp_count), ("dp", dp_count)))
+        d_in = sum_heads(d_in_part, mp_count)
+    attn_grads = attn_grads.astype(jnp.float32)
+    gains = jnp.split(gains, (width, 2 * width, 2 * width + HEAD_DIM))
+    d_in_norm, _ = norm_back(inputs, scale_in, attn_gain, d_in)
     grad_tokens = d_hidden + d_in_norm
-    totals = lax.psum(
-        (g_query, g_key, g_value, g_out, g_query_gain, g_key_gain, g_attn_gain, g_ffn_gain), "dp"
-    )
-    weight_terms = jnp.concatenate(
-        [
-            jnp.concatenate(
-                [
-                    lax.dot_general(
-                        normed_mid, d_gate, down_rows, preferred_element_type=jnp.float32
-                    ),
-                    lax.dot_general(
-                        normed_mid, d_up, down_rows, preferred_element_type=jnp.float32
-                    ),
-                ],
-                axis=1,
-            ),
-            lax.dot_general(grad_out, activated, down_rows, preferred_element_type=jnp.float32),
-        ],
-        axis=1,
-    )
-    mlp_grads = lax.psum_scatter(weight_terms, "dp", scatter_dimension=0, tiled=True)
-    grad_w_gate = mlp_grads[:, :mid_width]
-    grad_w_up = mlp_grads[:, mid_width : 2 * mid_width]
-    grad_w_down = mlp_grads[:, 2 * mid_width :].T
+    mlp_grads = mlp_sum.result()
+    value_at, out_at = query_width + key_width, query_width + 2 * key_width
     return (
         output,
         grad_tokens,
-        totals[6],
-        totals[0],
-        totals[1],
-        totals[2],
-        totals[4],
-        totals[5],
-        totals[3],
-        totals[7],
-        grad_w_gate,
-        grad_w_up,
-        grad_w_down,
+        gains[0],
+        attn_grads[:, :query_width],
+        attn_grads[:, query_width:value_at],
+        attn_grads[:, value_at:out_at],
+        gains[2],
+        gains[3],
+        attn_grads[:, out_at:].T,
+        gains[1],
+        mlp_grads[:, :mid_width],
+        mlp_grads[:, mid_width : 2 * mid_width],
+        mlp_grads[:, 2 * mid_width :].T,
     )
 
 
@@ -292,7 +680,7 @@
         P("dp", None),
     )
     return jax.shard_map(
-        shards,
+        functools.partial(shards, mesh.shape["dp"], mesh.shape["mp"]),
         mesh=mesh,
         in_specs=placed,
         out_specs=(

time: 571 us -> 269 us (0.47)
  waiting for transfers between devices: 429 us -> 97.9 us
  Pallas kernels: 0 us -> 45.3 us
  blocking collectives: 30.8 us -> 0 us
  starting transfers between devices: 0.51 us -> 24.4 us
  matrix products: 43.1 us -> 21.6 us
  local copies, waits for them, and re-layouts: 23.1 us -> 39.6 us
    reduce_scatter x1 -> x0, waiting for transfers between devices: 227 us -> none  [shards(): lax.psum_scatter(weight_terms, 'dp', scatter_dimension=0, tiled=True)]
    all_gather x3 -> x0, waiting for transfers between devices: 116 us -> none  [the longest x1 50.7 us: shards(): lax.all_gather(w_down, 'dp', axis=1, tiled=True)]
    ppermute x0 -> x25, waiting for transfers between devices: none -> 97.9 us  [the longest x4 38.1 us: send(): self.cw = lax.ppermute(self.cw, 'dp', self.moves[0])]
    psum x4 -> x0, waiting for transfers between devices: 84 us -> none  [the longest x1 35.4 us: shards(): hidden = inputs + lax.psum(head_part, 'mp')]
    pallas_call x0 -> x1, Pallas kernels: none -> 45.3 us  [finish(): pl.pallas_call(functools.partial(finish_kernel, dp_count), out_shape=(jax...]
    psum x2 -> x0, blocking collectives: 30.8 us -> none  [the longest x1 24.3 us: shards(): lax.psum((g_query, g_key, g_value, g_out, g_query_gain, g_key_gain, g_att...]
    ppermute x0 -> x25, starting transfers between devices: none -> 24.4 us  [the longest x3 6.97 us: step(): self.left = lax.ppermute(self.left, 'dp', ahead)]
    dot_general x18 -> x9, matrix products: 32 us -> 10.2 us  [the longest x1 1.55 us: shards(): lax.dot_general(normed_mid, d_both, down_rows, preferred_element_type=jnp...]
  transfers between devices with their start and end apart: 8 -> 25, of which waited for: 8 -> 16; matrix products, arithmetic and copies ran while one was open for 10% -> 14% of each run, Pallas kernels for 0% -> 0%
where the time goes in v1:
time: 269 us; the launch traced here: 268 us
  waiting for transfers between devices  97.9 us (36%)
  Pallas kernels  45.3 us (17%)
  local copies, waits for them, and re-layouts  39.6 us (15%)
  other arithmetic  26.7 us (10%)
  starting transfers between devices  24.4 us (9%)
  matrix products  21.6 us (8%)
  between operations  12.4 us (5%)
    pallas_call x1, Pallas kernels, finish(): pl.pallas_call(functools.partial(finish_kernel, dp_count), out_shape=(jax...  45.3 us
    ppermute x4, waiting for transfers between devices, send(): self.cw = lax.ppermute(self.cw, 'dp', self.moves[0])  38.1 us
    ppermute x3, waiting for transfers between devices, step(): self.left = lax.ppermute(self.left, 'dp', ahead)  28.6 us
    ppermute x4, waiting for transfers between devices, send(): self.ccw = lax.ppermute(self.ccw, 'dp', self.moves[1])  11.5 us
    ppermute x3, waiting for transfers between devices, sum_heads(): other = lax.ppermute(mine.astype(jnp.bfloat16), 'mp', across)  8.77 us
    ppermute x1, waiting for transfers between devices, step(): self.put(lax.ppermute(self.left[:half], 'dp', ahead), far)  8.45 us
    unnamed x119, local copies, waits for them, and re-layouts  7.7 us
    ppermute x3, starting transfers between devices, step(): self.left = lax.ppermute(self.left, 'dp', ahead)  6.97 us
  transfers between devices with their start and end apart: 25, of which 16 were waited for; matrix products, arithmetic and copies ran while one was open for 14% of the time, Pallas kernels for 0%

profile of v1, /device:TPU:0, one launch (start us, length us, event | category | flops | bytes accessed | tf_op | source)
XLA Modules:
  0.0 267.8 jit_solution(18076542328296753887)
XLA Ops:
  0.7 1.3 copy.127
  3.1 3.1 %collective-permute-start = (bf16[128,3456]{1,0:T(8,128)(2,1)S(1)}, bf16[128,3456]{1,0:T(8,128)(2,1)}, u32[]{:S(2)}, u32[]{:S(2)}) collective-permute-start(bf16[128,3456]{1,0:T(8,128)(2,1)S(1)} %pad_maximum_fusion.2), channel_id=1, source_target_pairs={{0,8},{8,16},{16,24},{24,28},{28,20},{20,12},{12,4},{4,0},{1,9},{9... | collective-permute-start | bytes 2654216 | tf_op jit(solution)/shard_map/ppermute | solution.py:168
  32.4 2.1 collective-permute-start.5
  36.5 2.0 collective-permute-start.3
  39.8 5.1 %collective-permute-done.3 = bf16[128,1024]{1,0:T(8,128)(2,1)S(1)} collective-permute-done((bf16[128,1024]{1,0:T(8,128)(2,1)S(1)}, bf16[128,1024]{1,0:T(8,128)(2,1)S(1)}, u32[]{:S(2)}, u32[]{:S(2)}) %collective-permute-start.3) | collective-permute-done | bytes 262176 | tf_op jit(solution)/shard_map/ppermute | solution.py:298
  45.1 9.8 %collective-permute-done.5 = bf16[128,3456]{1,0:T(8,128)(2,1)S(1)} collective-permute-done((bf16[128,3456]{1,0:T(8,128)(2,1)}, bf16[128,3456]{1,0:T(8,128)(2,1)S(1)}, u32[]{:S(2)}, u32[]{:S(2)}) %collective-permute-start.5) | collective-permute-done | bytes 884768 | tf_op jit(solution)/shard_map/ppermute | solution.py:168
  54.9 1.8 collective-permute-start.7
  57.4 18.8 %collective-permute-done.7 = bf16[128,3456]{1,0:T(8,128)(2,1)S(1)} collective-permute-done((bf16[128,3456]{1,0:T(8,128)(2,1)S(1)}, bf16[128,3456]{1,0:T(8,128)(2,1)S(1)}, u32[]{:S(2)}, u32[]{:S(2)}) %collective-permute-start.7) | collective-permute-done | bytes 884768 | tf_op jit(solution)/shard_map/ppermute | solution.py:168
  76.2 1.7 collective-permute-start.9
  78.8 8.4 %collective-permute-done.9 = bf16[64,3456]{1,0:T(8,128)(2,1)S(1)} collective-permute-done((bf16[64,3456]{1,0:T(8,128)(2,1)S(1)}, bf16[64,3456]{1,0:T(8,128)(2,1)S(1)}, u32[]{:S(2)}, u32[]{:S(2)}) %collective-permute-start.9) | collective-permute-done | bytes 442400 | tf_op jit(solution)/shard_map/ppermute | solution.py:182
  87.3 1.5 collective-permute-done.10
  88.9 1.5 fusion.2
  91.6 1.4 fusion
  93.0 1.6 convolution_convert_fusion
  97.2 1.6 collective-permute-start.15
  99.4 1.6 collective-permute-start.12
  101.0 8.3 %collective-permute-done.15 = bf16[64,3456]{1,0:T(8,128)(2,1)S(1)} collective-permute-done((bf16[64,3456]{1,0:T(8,128)(2,1)S(1)}, bf16[64,3456]{1,0:T(8,128)(2,1)S(1)}, u32[]{:S(2)}, u32[]{:S(2)}) %collective-permute-start.15) | collective-permute-done | bytes 442400 | tf_op jit(solution)/shard_map/ppermute | solution.py:226
  109.4 1.3 collective-permute-done.16
  110.7 1.6 collective-permute-start.17
  112.6 1.6 collective-permute-start.19
  114.2 3.6 %collective-permute-done.17 = bf16[128,1024]{1,0:T(8,128)(2,1)S(1)} collective-permute-done((bf16[128,1024]{1,0:T(8,128)(2,1)S(1)}, bf16[128,1024]{1,0:T(8,128)(2,1)S(1)}, u32[]{:S(2)}, u32[]{:S(2)}) %collective-permute-start.17) | collective-permute-done | bytes 262176 | tf_op jit(solution)/shard_map/ppermute | solution.py:298
  123.5 9.3 %collective-permute-done.19 = bf16[128,3456]{1,0:T(8,128)(2,1)S(1)} collective-permute-done((bf16[128,3456]{1,0:T(8,128)(2,1)S(1)}, bf16[128,3456]{1,0:T(8,128)(2,1)S(1)}, u32[]{:S(2)}, u32[]{:S(2)}) %collective-permute-start.19) | collective-permute-done | bytes 884768 | tf_op jit(solution)/shard_map/ppermute | solution.py:226
  132.8 7.6 %collective-permute-done.20 = bf16[128,3456]{1,0:T(8,128)(2,1)S(1)} collective-permute-done((bf16[128,3456]{1,0:T(8,128)(2,1)S(1)}, bf16[128,3456]{1,0:T(8,128)(2,1)S(1)}, u32[]{:S(2)}, u32[]{:S(2)}) %collective-permute-start.20) | collective-permute-done | bytes 884768 | tf_op jit(solution)/shard_map/ppermute | solution.py:227
  142.1 2.3 fusion.16
  144.4 2.6 fusion.13
  147.0 1.3 convolution_bitcast_fusion.3
  148.4 2.9 %add_convert_fusion.2 = (bf16[128,3456]{1,0:T(8,128)(2,1)}, bf16[128,3456]{1,0:T(8,128)(2,1)}) fusion(bf16[128,3456]{1,0:T(8,128)(2,1)S(1)} %copy-done.23, s32[]{:T(128)S(6)} %select_n.253, bf16[1024,1152]{1,0:T(8,128)(2,1)S(1)} %fusion.4, bf16[1024,2304]{1,0:T(8,128)(2,1)} %copy-done.1, bf16[128,3456]{1,0:T(8,128)(2,1)S(1)} %copy-done.20, s32[]{:T(128)S(6)} %select_n.256), kind=kLoop, calls=%fused_computation.41 | loop fusion | flops 6193152 | bytes 10616840 | tf_op jit(solution)/shard_map/convert_element_type | solution.py:223
  151.4 1.6 collective-permute-start.21
  154.6 1.7 copy.156
  156.3 1.7 copy.155
  158.0 1.6 copy.149
  162.0 1.8 fusion.55
  163.8 1.7 fusion.64
  166.8 5.6 %collective-permute-done.21 = bf16[128,3456]{1,0:T(8,128)(2,1)} collective-permute-done((bf16[128,3456]{1,0:T(8,128)(2,1)}, bf16[128,3456]{1,0:T(8,128)(2,1)}, u32[]{:S(2)}, u32[]{:S(2)}) %collective-permute-start.21) | collective-permute-done | bytes 884768 | tf_op jit(solution)/shard_map/ppermute | solution.py:226
  173.7 1.5 multiply_add_fusion
  175.2 1.9 copy.153
  177.1 1.7 pad_maximum_fusion.7
  180.5 1.8 copy.140
  182.3 1.8 copy.135
  184.2 3.6 %add_convert_fusion = (bf16[128,3456]{1,0:T(8,128)(2,1)}, bf16[128,3456]{1,0:T(8,128)(2,1)}) fusion(bf16[128,3456]{1,0:T(8,128)(2,1)} %collective-permute-done.22, s32[]{:T(128)S(6)} %select_n.247, bf16[1024,1152]{1,0:T(8,128)(2,1)S(1)} %fusion.4, bf16[1024,2304]{1,0:T(8,128)(2,1)} %copy-done.1, bf16[128,3456]{1,0:T(8,128)(2,1)} %collective-permute-done.21, ...), kind=kLoop, calls=%fused_computation.39 | loop fusion | flops 6193152 | bytes 10616840 | tf_op jit(solution)/shard_map/convert_element_type | solution.py:223
  187.8 1.6 collective-permute-start.23
  191.0 1.5 convolution_convert_fusion.2
  192.7 14.9 %collective-permute-done.23 = bf16[128,3456]{1,0:T(8,128)(2,1)S(1)} collective-permute-done((bf16[128,3456]{1,0:T(8,128)(2,1)}, bf16[128,3456]{1,0:T(8,128)(2,1)S(1)}, u32[]{:S(2)}, u32[]{:S(2)}) %collective-permute-start.23) | collective-permute-done | bytes 884768 | tf_op jit(solution)/shard_map/ppermute | solution.py:226
  207.5 1.3 collective-permute-done.24
  208.9 45.3 %shard_map.273 = (bf16[1024,768]{1,0:T(8,128)(2,1)S(1)}, f32[256,1024]{1,0:T(8,128)S(1)}, f32[24,128]{1,0:T(8,128)S(1)}) custom-call(bf16[1024,768]{1,0:T(8,128)(2,1)S(1)} %pad_maximum_fusion.terms, f32[256,1024]{1,0:T(8,128)S(1)} %get-tuple-element.164.part, f32[24,128]{1,0:T(8,128)S(1)} %pad_bitcast_fusion.vector), custom_call_target="tpu_custom_call" | custom-call | tf_op jit(solution)/shard_map/pallas_call | solution.py:494
  258.1 1.3 fusion.21
  261.2 2.5 copy.158
  263.7 1.9 convert_add_fusion.1
  (252 shorter events, 51.3 us)
Async XLA Ops:
  0.6 31.3 %copy-start = (bf16[256,1024]{1,0:T(8,128)(2,1)S(1)}, bf16[256,1024]{1,0:T(8,128)(2,1)}, u32[]{:S(2)}) copy-start(bf16[256,1024]{1,0:T(8,128)(2,1)} %param.26) | copy-start | bytes 1572868
  0.7 5.9 %copy-start.39 = (bf16[1024,128]{1,0:T(8,128)(2,1)S(1)}, bf16[1024,128]{1,0:T(8,128)(2,1)}, u32[]{:S(2)}) copy-start(bf16[1024,128]{1,0:T(8,128)(2,1)} %param.23) | copy-start | bytes 786436
  0.7 6.0 %copy-start.47 = (f32[1024]{0:T(1024)S(1)}, f32[1024]{0:T(1024)}, u32[]{:S(2)}) copy-start(f32[1024]{0:T(1024)} %param.20) | copy-start | bytes 12292
  3.1 28.8 %collective-permute-start = (bf16[128,3456]{1,0:T(8,128)(2,1)S(1)}, bf16[128,3456]{1,0:T(8,128)(2,1)}, u32[]{:S(2)}, u32[]{:S(2)}) collective-permute-start(bf16[128,3456]{1,0:T(8,128)(2,1)S(1)} %pad_maximum_fusion.2), channel_id=1, source_target_pairs={{0,8},{8,16},{16,24},{24,28},{28,20},{20,12},{12,4},{4,0},{1,9},{9... | collective-permute-start | bytes 2654216 | tf_op jit(solution)/shard_map/ppermute | solution.py:168
  6.2 25.7 %collective-permute-start.1 = (bf16[128,3456]{1,0:T(8,128)(2,1)S(1)}, bf16[128,3456]{1,0:T(8,128)(2,1)}, u32[]{:S(2)}, u32[]{:S(2)}) collective-permute-start(bf16[128,3456]{1,0:T(8,128)(2,1)S(1)} %pad_maximum_fusion.2), channel_id=1, source_target_pairs={{8,0},{16,8},{24,16},{28,24},{20,28},{12,20},{4,12},{0,4},{9,1},{1... | collective-permute-start | bytes 2654216 | tf_op jit(solution)/shard_map/ppermute | solution.py:169
  6.5 8.3 %copy-start.45 = (s32[8]{0:T(128)S(1)}, s32[8]{0:T(128)}, u32[]{:S(2)}) copy-start(s32[8]{0:T(128)} %constant.222.clone) | copy-start | bytes 100
  6.5 14.3 %copy-start.51 = (f32[256]{0:T(256)}, f32[256]{0:T(256)S(1)}, u32[]{:S(2)}) copy-start(f32[256]{0:T(256)S(1)} %add_rsqrt_fusion.3) | copy-start | bytes 3076
  7.2 16.4 %copy-start.49 = (f32[64]{0:T(128)S(1)}, f32[64]{0:T(128)}, u32[]{:S(2)}) copy-start(f32[64]{0:T(128)} %param.24) | copy-start | bytes 772
  7.2 16.6 %copy-start.53 = (f32[64]{0:T(128)S(1)}, f32[64]{0:T(128)}, u32[]{:S(2)}) copy-start(f32[64]{0:T(128)} %param.25) | copy-start | bytes 772
  20.8 6.3 %copy-start.7 = (f32[256,256]{0,1:T(8,128)}, f32[256,256]{0,1:T(8,128)S(1)}, u32[]{:S(2)}) copy-start(f32[256,256]{0,1:T(8,128)S(1)} %copy.130) | copy-start | bytes 786436
  24.2 7.7 %copy-start.32 = (bf16[256,4,32]{0,2,1:T(8,128)(2,1)}, bf16[256,4,32]{0,2,1:T(8,128)(2,1)S(1)}, u32[]{:S(2)}) copy-start(bf16[256,4,32]{0,2,1:T(8,128)(2,1)S(1)} %get-tuple-element.137) | copy-start | bytes 196612
  24.2 7.7 %copy-start.34 = (bf16[256,4,32]{0,2,1:T(8,128)(2,1)}, bf16[256,4,32]{0,2,1:T(8,128)(2,1)S(1)}, u32[]{:S(2)}) copy-start(bf16[256,4,32]{0,2,1:T(8,128)(2,1)S(1)} %get-tuple-element.138) | copy-start | bytes 196612
  24.9 7.0 %copy-start.42 = (bf16[256,2,32]{0,2,1:T(8,128)(2,1)}, bf16[256,2,32]{0,2,1:T(8,128)(2,1)S(1)}, u32[]{:S(2)}) copy-start(bf16[256,2,32]{0,2,1:T(8,128)(2,1)S(1)} %get-tuple-element.143) | copy-start | bytes 98308
  32.3 4.1 %collective-permute-start.2 = (bf16[128,1024]{1,0:T(8,128)(2,1)S(1)}, bf16[128,1024]{1,0:T(8,128)(2,1)S(1)}, u32[]{:S(2)}, u32[]{:S(2)}) collective-permute-start(bf16[128,1024]{1,0:T(8,128)(2,1)S(1)} %dynamic-slice_convert_fusion.2), channel_id=1, source_target_pairs={{0,1},{1,0},{2,3},{3,2},{4,5},{5,4},{6,7},{7,6},{8,9},{9,8},{10,11... | collective-permute-start | bytes 786440 | tf_op jit(solution)/shard_map/ppermute | solution.py:296
  32.4 22.5 %collective-permute-start.5 = (bf16[128,3456]{1,0:T(8,128)(2,1)}, bf16[128,3456]{1,0:T(8,128)(2,1)S(1)}, u32[]{:S(2)}, u32[]{:S(2)}) collective-permute-start(bf16[128,3456]{1,0:T(8,128)(2,1)} %collective-permute-done), channel_id=1, source_target_pairs={{0,8},{8,16},{16,24},{24,28},{28,20},{20,12},{12,4},{4,0},{1,9},{9... | collective-permute-start | bytes 2654216 | tf_op jit(solution)/shard_map/ppermute | solution.py:168
  34.5 22.2 %collective-permute-start.6 = (bf16[128,3456]{1,0:T(8,128)(2,1)}, bf16[128,3456]{1,0:T(8,128)(2,1)S(1)}, u32[]{:S(2)}, u32[]{:S(2)}) collective-permute-start(bf16[128,3456]{1,0:T(8,128)(2,1)} %collective-permute-done.1), channel_id=1, source_target_pairs={{8,0},{16,8},{24,16},{28,24},{20,28},{12,20},{4,12},{0,4},{9,1},{1... | collective-permute-start | bytes 2654216 | tf_op jit(solution)/shard_map/ppermute | solution.py:169
  36.5 8.4 %collective-permute-start.3 = (bf16[128,1024]{1,0:T(8,128)(2,1)S(1)}, bf16[128,1024]{1,0:T(8,128)(2,1)S(1)}, u32[]{:S(2)}, u32[]{:S(2)}) collective-permute-start(bf16[128,1024]{1,0:T(8,128)(2,1)S(1)} %fusion.48), channel_id=1, source_target_pairs={{0,2},{1,3},{2,0},{3,1},{4,6},{5,7},{6,4},{7,5},{8,10},{9,11},{10,... | collective-permute-start | bytes 786440 | tf_op jit(solution)/shard_map/ppermute | solution.py:298
  45.0 12.1 %collective-permute-start.4 = (f32[128,1024]{1,0:T(8,128)S(1)}, f32[128,1024]{1,0:T(8,128)S(1)}, u32[]{:S(2)}, u32[]{:S(2)}) collective-permute-start(f32[128,1024]{1,0:T(8,128)S(1)} %convert_add_fusion.4), channel_id=1, source_target_pairs={{0,1},{1,0},{2,3},{3,2},{4,5},{5,4},{6,7},{7,6},{8,9},{9,8},{10,11... | collective-permute-start | bytes 1572872 | tf_op jit(solution)/shard_map/ppermute | solution.py:300
  54.9 21.3 %collective-permute-start.7 = (bf16[128,3456]{1,0:T(8,128)(2,1)S(1)}, bf16[128,3456]{1,0:T(8,128)(2,1)S(1)}, u32[]{:S(2)}, u32[]{:S(2)}) collective-permute-start(bf16[128,3456]{1,0:T(8,128)(2,1)S(1)} %collective-permute-done.5), channel_id=1, source_target_pairs={{0,8},{8,16},{16,24},{24,28},{28,20},{20,12},{12,4},{4,0},{1,9},{9... | collective-permute-start | bytes 2654216 | tf_op jit(solution)/shard_map/ppermute | solution.py:168
  56.7 21.3 %collective-permute-start.8 = (bf16[128,3456]{1,0:T(8,128)(2,1)S(1)}, bf16[128,3456]{1,0:T(8,128)(2,1)S(1)}, u32[]{:S(2)}, u32[]{:S(2)}) collective-permute-start(bf16[128,3456]{1,0:T(8,128)(2,1)S(1)} %collective-permute-done.6), channel_id=1, source_target_pairs={{8,0},{16,8},{24,16},{28,24},{20,28},{12,20},{4,12},{0,4},{9,1},{1... | collective-permute-start | bytes 2654216 | tf_op jit(solution)/shard_map/ppermute | solution.py:169
  76.2 11.0 %collective-permute-start.9 = (bf16[64,3456]{1,0:T(8,128)(2,1)S(1)}, bf16[64,3456]{1,0:T(8,128)(2,1)S(1)}, u32[]{:S(2)}, u32[]{:S(2)}) collective-permute-start(bf16[64,3456]{1,0:T(8,128)(2,1)S(1)} %slice.117), channel_id=1, source_target_pairs={{0,8},{8,16},{16,24},{24,28},{28,20},{20,12},{12,4},{4,0},{1,9},{9... | collective-permute-start | bytes 1327112 | tf_op jit(solution)/shard_map/ppermute | solution.py:182
  78.0 10.8 %copy-start.40 = (f32[1024]{0:T(1024)S(1)}, f32[1024]{0:T(1024)}, u32[]{:S(2)}) copy-start(f32[1024]{0:T(1024)} %param.27) | copy-start | bytes 12292
  78.0 10.8 %collective-permute-start.10 = (bf16[64,3456]{1,0:T(8,128)(2,1)S(1)}, bf16[64,3456]{1,0:T(8,128)(2,1)S(1)}, u32[]{:S(2)}, u32[]{:S(2)}) collective-permute-start(bf16[64,3456]{1,0:T(8,128)(2,1)S(1)} %slice.118), channel_id=1, source_target_pairs={{8,0},{16,8},{24,16},{28,24},{20,28},{12,20},{4,12},{0,4},{9,1},{1... | collective-permute-start | bytes 1327112 | tf_op jit(solution)/shard_map/ppermute | solution.py:183
  94.6 17.7 %copy-start.1 = (bf16[1024,2304]{1,0:T(8,128)(2,1)}, bf16[1024,2304]{1,0:T(8,128)(2,1)S(1)}, u32[]{:S(2)}) copy-start(bf16[1024,2304]{1,0:T(8,128)(2,1)S(1)} %convolution_convert_fusion) | copy-start | bytes 14155780
  95.5 88.6 %copy-start.2 = (bf16[1024,1152]{1,0:T(8,128)(2,1)}, bf16[1024,1152]{1,0:T(8,128)(2,1)S(1)}, u32[]{:S(2)}) copy-start(bf16[1024,1152]{1,0:T(8,128)(2,1)S(1)} %fusion.4) | copy-start | bytes 7077892
  96.4 4.5 %collective-permute-start.14 = (bf16[128,1024]{1,0:T(8,128)(2,1)S(1)}, bf16[128,1024]{1,0:T(8,128)(2,1)S(1)}, u32[]{:S(2)}, u32[]{:S(2)}) collective-permute-start(bf16[128,1024]{1,0:T(8,128)(2,1)S(1)} %dynamic-slice_convert_fusion), channel_id=1, source_target_pairs={{0,1},{1,0},{2,3},{3,2},{4,5},{5,4},{6,7},{7,6},{8,9},{9,8},{10,11... | collective-permute-start | bytes 786440 | tf_op jit(solution)/shard_map/ppermute | solution.py:296
  96.5 2.8 %collective-permute-start.11 = (bf16[128,1024]{1,0:T(8,128)(2,1)S(1)}, bf16[128,1024]{1,0:T(8,128)(2,1)S(1)}, u32[]{:S(2)}, u32[]{:S(2)}) collective-permute-start(bf16[128,1024]{1,0:T(8,128)(2,1)S(1)} %dynamic-slice_convert_fusion.1), channel_id=1, source_target_pairs={{0,1},{1,0},{2,3},{3,2},{4,5},{5,4},{6,7},{7,6},{8,9},{9,8},{10,11... | collective-permute-start | bytes 786440 | tf_op jit(solution)/shard_map/ppermute | solution.py:296
  97.2 12.2 %collective-permute-start.15 = (bf16[64,3456]{1,0:T(8,128)(2,1)S(1)}, bf16[64,3456]{1,0:T(8,128)(2,1)S(1)}, u32[]{:S(2)}, u32[]{:S(2)}) collective-permute-start(bf16[64,3456]{1,0:T(8,128)(2,1)S(1)} %get-tuple-element.120), channel_id=1, source_target_pairs={{0,8},{8,16},{16,24},{24,28},{28,20},{20,12},{12,4},{4,0},{1,9},{9... | collective-permute-start | bytes 1327112 | tf_op jit(solution)/shard_map/ppermute | solution.py:226
  98.9 11.8 %collective-permute-start.16 = (bf16[64,3456]{1,0:T(8,128)(2,1)S(1)}, bf16[64,3456]{1,0:T(8,128)(2,1)S(1)}, u32[]{:S(2)}, u32[]{:S(2)}) collective-permute-start(bf16[64,3456]{1,0:T(8,128)(2,1)S(1)} %get-tuple-element.121), channel_id=1, source_target_pairs={{8,0},{16,8},{24,16},{28,24},{20,28},{12,20},{4,12},{0,4},{9,1},{1... | collective-permute-start | bytes 1327112 | tf_op jit(solution)/shard_map/ppermute | solution.py:227
  99.4 18.6 %collective-permute-start.12 = (bf16[128,1024]{1,0:T(8,128)(2,1)S(1)}, bf16[128,1024]{1,0:T(8,128)(2,1)S(1)}, u32[]{:S(2)}, u32[]{:S(2)}) collective-permute-start(bf16[128,1024]{1,0:T(8,128)(2,1)S(1)} %fusion.49), channel_id=1, source_target_pairs={{0,2},{1,3},{2,0},{3,1},{4,6},{5,7},{6,4},{7,5},{8,10},{9,11},{10,... | collective-permute-start | bytes 786440 | tf_op jit(solution)/shard_map/ppermute | solution.py:298
  110.7 7.1 %collective-permute-start.17 = (bf16[128,1024]{1,0:T(8,128)(2,1)S(1)}, bf16[128,1024]{1,0:T(8,128)(2,1)S(1)}, u32[]{:S(2)}, u32[]{:S(2)}) collective-permute-start(bf16[128,1024]{1,0:T(8,128)(2,1)S(1)} %convert_element_type.223), channel_id=1, source_target_pairs={{0,2},{1,3},{2,0},{3,1},{4,6},{5,7},{6,4},{7,5},{8,10},{9,11},{10,... | collective-permute-start | bytes 786440 | tf_op jit(solution)/shard_map/ppermute | solution.py:298
  112.6 20.2 %collective-permute-start.19 = (bf16[128,3456]{1,0:T(8,128)(2,1)S(1)}, bf16[128,3456]{1,0:T(8,128)(2,1)S(1)}, u32[]{:S(2)}, u32[]{:S(2)}) collective-permute-start(bf16[128,3456]{1,0:T(8,128)(2,1)S(1)} %pad_maximum_fusion.3), channel_id=1, source_target_pairs={{0,8},{8,16},{16,24},{24,28},{28,20},{20,12},{12,4},{4,0},{1,9},{9... | collective-permute-start | bytes 2654216 | tf_op jit(solution)/shard_map/ppermute | solution.py:226
  117.9 2.0 collective-permute-start.18
  118.1 2.5 collective-permute-start.13
  118.7 21.6 %collective-permute-start.20 = (bf16[128,3456]{1,0:T(8,128)(2,1)S(1)}, bf16[128,3456]{1,0:T(8,128)(2,1)S(1)}, u32[]{:S(2)}, u32[]{:S(2)}) collective-permute-start(bf16[128,3456]{1,0:T(8,128)(2,1)S(1)} %pad_maximum_fusion.4), channel_id=1, source_target_pairs={{8,0},{16,8},{24,16},{28,24},{20,28},{12,20},{4,12},{0,4},{9,1},{1... | collective-permute-start | bytes 2654216 | tf_op jit(solution)/shard_map/ppermute | solution.py:227
  123.4 16.9 %copy-start.31 = (bf16[256,256]{0,1:T(8,128)(2,1)}, bf16[256,256]{0,1:T(8,128)(2,1)S(1)}, u32[]{:S(2)}) copy-start(bf16[256,256]{0,1:T(8,128)(2,1)S(1)} %convolution_convert_fusion.4) | copy-start | bytes 393220
  132.8 7.6 %copy-start.19 = (bf16[128,3456]{1,0:T(8,128)(2,1)}, bf16[128,3456]{1,0:T(8,128)(2,1)S(1)}, u32[]{:S(2)}) copy-start(bf16[128,3456]{1,0:T(8,128)(2,1)S(1)} %collective-permute-done.19) | copy-start | bytes 2654212
  142.1 6.2 %copy-start.25 = (f32[256,32]{0,1:T(8,128)S(1)}, f32[256,32]{0,1:T(8,128)}, u32[]{:S(2)}) copy-start(f32[256,32]{0,1:T(8,128)} %copy-done.24) | copy-start | bytes 98308
  142.1 6.3 %copy-start.27 = (f32[256,32]{0,1:T(8,128)S(1)}, f32[256,32]{0,1:T(8,128)}, u32[]{:S(2)}) copy-start(f32[256,32]{0,1:T(8,128)} %copy-done.26) | copy-start | bytes 98308
  142.1 6.3 %copy-start.20 = (bf16[128,3456]{1,0:T(8,128)(2,1)S(1)}, bf16[128,3456]{1,0:T(8,128)(2,1)}, u32[]{:S(2)}) copy-start(bf16[128,3456]{1,0:T(8,128)(2,1)} %copy-done.19) | copy-start | bytes 2654212
  142.1 6.3 %copy-start.23 = (bf16[128,3456]{1,0:T(8,128)(2,1)S(1)}, bf16[128,3456]{1,0:T(8,128)(2,1)}, u32[]{:S(2)}) copy-start(bf16[128,3456]{1,0:T(8,128)(2,1)} %copy-done.22) | copy-start | bytes 2654212
  148.4 13.6 %copy-start.48 = (f32[512]{0:T(512)S(1)}, f32[512]{0:T(512)}, u32[]{:S(2)}) copy-start(f32[512]{0:T(512)} %rsqrt.45) | copy-start | bytes 6148
  151.4 21.0 %collective-permute-start.21 = (bf16[128,3456]{1,0:T(8,128)(2,1)}, bf16[128,3456]{1,0:T(8,128)(2,1)}, u32[]{:S(2)}, u32[]{:S(2)}) collective-permute-start(bf16[128,3456]{1,0:T(8,128)(2,1)} %get-tuple-element.118), channel_id=1, source_target_pairs={{0,8},{8,16},{16,24},{24,28},{28,20},{20,12},{12,4},{4,0},{1,9},{9... | collective-permute-start | bytes 2654216 | tf_op jit(solution)/shard_map/ppermute | solution.py:226
  152.9 20.8 %collective-permute-start.22 = (bf16[128,3456]{1,0:T(8,128)(2,1)}, bf16[128,3456]{1,0:T(8,128)(2,1)}, u32[]{:S(2)}, u32[]{:S(2)}) collective-permute-start(bf16[128,3456]{1,0:T(8,128)(2,1)} %get-tuple-element.117), channel_id=1, source_target_pairs={{8,0},{16,8},{24,16},{28,24},{20,28},{12,20},{4,12},{0,4},{9,1},{1... | collective-permute-start | bytes 2654216 | tf_op jit(solution)/shard_map/ppermute | solution.py:227
  184.1 5.9 %copy-start.8 = (f32[256,4,32]{2,1,0:T(4,128)S(1)}, f32[256,4,32]{2,1,0:T(4,128)}, u32[]{:S(2)}) copy-start(f32[256,4,32]{2,1,0:T(4,128)} %copy.153) | copy-start | bytes 393220
  187.8 19.8 %collective-permute-start.23 = (bf16[128,3456]{1,0:T(8,128)(2,1)}, bf16[128,3456]{1,0:T(8,128)(2,1)S(1)}, u32[]{:S(2)}, u32[]{:S(2)}) collective-permute-start(bf16[128,3456]{1,0:T(8,128)(2,1)} %get-tuple-element.116), channel_id=1, source_target_pairs={{0,8},{8,16},{16,24},{24,28},{28,20},{20,12},{12,4},{4,0},{1,9},{9... | collective-permute-start | bytes 2654216 | tf_op jit(solution)/shard_map/ppermute | solution.py:226
  189.3 19.6 %collective-permute-start.24 = (bf16[128,3456]{1,0:T(8,128)(2,1)}, bf16[128,3456]{1,0:T(8,128)(2,1)}, u32[]{:S(2)}, u32[]{:S(2)}) collective-permute-start(bf16[128,3456]{1,0:T(8,128)(2,1)} %get-tuple-element.115), channel_id=1, source_target_pairs={{8,0},{16,8},{24,16},{28,24},{20,28},{12,20},{4,12},{0,4},{9,1},{1... | collective-permute-start | bytes 2654216 | tf_op jit(solution)/shard_map/ppermute | solution.py:227
  207.5 47.7 %copy-start.21 = (bf16[128,3456]{1,0:T(8,128)(2,1)}, bf16[128,3456]{1,0:T(8,128)(2,1)S(1)}, u32[]{:S(2)}) copy-start(bf16[128,3456]{1,0:T(8,128)(2,1)S(1)} %collective-permute-done.23) | copy-start | bytes 2654212
  (34 other events, 123.4 us)

commit v2 on v1

--- a/solution.py
+++ b/solution.py
@@ -243,14 +243,6 @@
             self.cw = self.plus(self.term(step), self.cw)
             self.ccw = self.plus(self.term(-step), self.ccw)
         self.send()
-
-    def finished(self, value):
-        if not self.ring:
-            return value
-        while self.left:
-            self.step()
-        value, self.cw, self.ccw = lax.optimization_barrier((value, self.cw, self.ccw))
-        return value
 
     def tie(self, value):
         if not self.ring or self.left == 0:
@@ -623,6 +615,7 @@
     d_query_half = d_query.astype(jnp.bfloat16).reshape(token_count, -1)
     d_key_half = d_key.astype(jnp.bfloat16).reshape(token_count, -1)
     d_value_half = d_value.reshape(token_count, -1)
+    mlp_grads = mlp_sum.result()
     d_heads = jnp.concatenate([d_query_half, d_key_half, d_value_half], axis=1)
     g_heads = lax.dot_general(normed_in, d_heads, down_rows, preferred_element_type=jnp.float32)
     d_in_part = lax.dot_general(d_heads, w_heads, across, preferred_element_type=jnp.float32)
@@ -631,7 +624,6 @@
     attn_terms = jnp.concatenate(
         [g_heads.astype(jnp.bfloat16), g_out.astype(jnp.bfloat16)], axis=1
     )
-    attn_terms = mlp_sum.finished(attn_terms)
     if dp_count in (4, 8, 16) and mp_count == 4:
         attn_grads, d_in, gains = finish(attn_terms, d_in_part, vector, dp_count)
     else:
@@ -643,7 +635,6 @@
     gains = jnp.split(gains, (width, 2 * width, 2 * width + HEAD_DIM))
     d_in_norm, _ = norm_back(inputs, scale_in, attn_gain, d_in)
     grad_tokens = d_hidden + d_in_norm
-    mlp_grads = mlp_sum.result()
     value_at, out_at = query_width + key_width, query_width + 2 * key_width
     return (
         output,

time: 269 us -> 256 us (0.952)
  local copies, waits for them, and re-layouts: 39.6 us -> 33.8 us
  waiting for transfers between devices: 97.9 us -> 94.5 us
  other arithmetic: 26.7 us -> 23.9 us
    ppermute x4, waiting for transfers between devices: 38.1 us -> 29.6 us  [send(): self.cw = lax.ppermute(self.cw, 'dp', self.moves[0])]
    ppermute x4, waiting for transfers between devices: 11.5 us -> 16.6 us  [send(): self.ccw = lax.ppermute(self.ccw, 'dp', self.moves[1])]
    mul x4, local copies, waits for them, and re-layouts: 3.26 us -> 0.25 us  [norm_back(): values * scale_fac * scale_fac * scale_fac]
    unnamed x119 -> x125, local copies, waits for them, and re-layouts: 7.7 us -> 9.94 us
  transfers between devices with their start and end apart: 25 -> 25, of which waited for: 16 -> 16; matrix products, arithmetic and copies ran while one was open for 14% -> 15% of each run, Pallas kernels for 0% -> 0%
where the time goes in v2:
time: 256 us; the launch traced here: 255 us
  waiting for transfers between devices  94.5 us (37%)
  Pallas kernels  44.7 us (17%)
  local copies, waits for them, and re-layouts  33.8 us (13%)
  starting transfers between devices  24.8 us (10%)
  other arithmetic  23.9 us (9%)
  matrix products  21.4 us (8%)
  between operations  12.4 us (5%)
    pallas_call x1, Pallas kernels, finish(): pl.pallas_call(functools.partial(finish_kernel, dp_count), out_shape=(jax...  44.7 us
    ppermute x4, waiting for transfers between devices, send(): self.cw = lax.ppermute(self.cw, 'dp', self.moves[0])  29.6 us
    ppermute x3, waiting for transfers between devices, step(): self.left = lax.ppermute(self.left, 'dp', ahead)  28.6 us
    ppermute x4, waiting for transfers between devices, send(): self.ccw = lax.ppermute(self.ccw, 'dp', self.moves[1])  16.6 us
    unnamed x125, local copies, waits for them, and re-layouts  9.94 us
    ppermute x3, waiting for transfers between devices, sum_heads(): other = lax.ppermute(mine.astype(jnp.bfloat16), 'mp', across)  8.75 us
    ppermute x1, waiting for transfers between devices, step(): self.put(lax.ppermute(self.left[:half], 'dp', ahead), far)  8.44 us
    ppermute x3, starting transfers between devices, step(): self.left = lax.ppermute(self.left, 'dp', ahead)  6.98 us
  transfers between devices with their start and end apart: 25, of which 16 were waited for; matrix products, arithmetic and copies ran while one was open for 15% of the time, Pallas kernels for 0%

profile of v2, /device:TPU:0, one launch (start us, length us, event | category | flops | bytes accessed | tf_op | source)
XLA Modules:
  0.0 255.4 jit_solution(5177175119423258608)
XLA Ops:
  0.7 1.3 copy.127
  3.1 3.1 %collective-permute-start = (bf16[128,3456]{1,0:T(8,128)(2,1)S(1)}, bf16[128,3456]{1,0:T(8,128)(2,1)}, u32[]{:S(2)}, u32[]{:S(2)}) collective-permute-start(bf16[128,3456]{1,0:T(8,128)(2,1)S(1)} %pad_maximum_fusion.2), channel_id=1, source_target_pairs={{0,8},{8,16},{16,24},{24,28},{28,20},{20,12},{12,4},{4,0},{1,9},{9... | collective-permute-start | bytes 2654216 | tf_op jit(solution)/shard_map/ppermute | solution.py:168
  30.2 1.3 fusion.78
  34.1 2.1 collective-permute-start.5
  36.8 1.3 constant_dynamic-update-slice_fusion.7
  38.2 2.0 collective-permute-start.3
  40.2 1.3 constant_dynamic-update-slice_fusion.6
  41.5 5.1 %collective-permute-done.3 = bf16[128,1024]{1,0:T(8,128)(2,1)S(1)} collective-permute-done((bf16[128,1024]{1,0:T(8,128)(2,1)S(1)}, bf16[128,1024]{1,0:T(8,128)(2,1)S(1)}, u32[]{:S(2)}, u32[]{:S(2)}) %collective-permute-start.3) | collective-permute-done | bytes 262176 | tf_op jit(solution)/shard_map/ppermute | solution.py:290
  46.8 9.8 %collective-permute-done.5 = bf16[128,3456]{1,0:T(8,128)(2,1)S(1)} collective-permute-done((bf16[128,3456]{1,0:T(8,128)(2,1)}, bf16[128,3456]{1,0:T(8,128)(2,1)S(1)}, u32[]{:S(2)}, u32[]{:S(2)}) %collective-permute-start.5) | collective-permute-done | bytes 884768 | tf_op jit(solution)/shard_map/ppermute | solution.py:168
  56.6 1.8 collective-permute-start.7
  59.1 18.8 %collective-permute-done.7 = bf16[128,3456]{1,0:T(8,128)(2,1)S(1)} collective-permute-done((bf16[128,3456]{1,0:T(8,128)(2,1)S(1)}, bf16[128,3456]{1,0:T(8,128)(2,1)S(1)}, u32[]{:S(2)}, u32[]{:S(2)}) %collective-permute-start.7) | collective-permute-done | bytes 884768 | tf_op jit(solution)/shard_map/ppermute | solution.py:168
  77.9 1.8 collective-permute-start.9
  80.5 8.4 %collective-permute-done.9 = bf16[64,3456]{1,0:T(8,128)(2,1)S(1)} collective-permute-done((bf16[64,3456]{1,0:T(8,128)(2,1)S(1)}, bf16[64,3456]{1,0:T(8,128)(2,1)S(1)}, u32[]{:S(2)}, u32[]{:S(2)}) %collective-permute-start.9) | collective-permute-done | bytes 442400 | tf_op jit(solution)/shard_map/ppermute | solution.py:182
  89.0 1.5 collective-permute-done.10
  90.6 1.5 fusion.2
  92.1 1.2 multiply_convert_fusion.1
  93.3 1.4 fusion
  94.7 1.5 convolution_convert_fusion
  98.9 1.6 collective-permute-start.15
  101.1 1.6 collective-permute-start.12
  102.7 8.3 %collective-permute-done.15 = bf16[64,3456]{1,0:T(8,128)(2,1)S(1)} collective-permute-done((bf16[64,3456]{1,0:T(8,128)(2,1)S(1)}, bf16[64,3456]{1,0:T(8,128)(2,1)S(1)}, u32[]{:S(2)}, u32[]{:S(2)}) %collective-permute-start.15) | collective-permute-done | bytes 442400 | tf_op jit(solution)/shard_map/ppermute | solution.py:226
  111.1 1.3 collective-permute-done.16
  112.4 1.6 collective-permute-start.17
  114.3 1.6 collective-permute-start.19
  115.9 3.6 %collective-permute-done.17 = bf16[128,1024]{1,0:T(8,128)(2,1)S(1)} collective-permute-done((bf16[128,1024]{1,0:T(8,128)(2,1)S(1)}, bf16[128,1024]{1,0:T(8,128)(2,1)S(1)}, u32[]{:S(2)}, u32[]{:S(2)}) %collective-permute-start.17) | collective-permute-done | bytes 262176 | tf_op jit(solution)/shard_map/ppermute | solution.py:290
  122.3 1.4 subtract_add_fusion
  123.7 1.2 convolution_convert_fusion.3
  125.3 9.2 %collective-permute-done.19 = bf16[128,3456]{1,0:T(8,128)(2,1)S(1)} collective-permute-done((bf16[128,3456]{1,0:T(8,128)(2,1)S(1)}, bf16[128,3456]{1,0:T(8,128)(2,1)S(1)}, u32[]{:S(2)}, u32[]{:S(2)}) %collective-permute-start.19) | collective-permute-done | bytes 884768 | tf_op jit(solution)/shard_map/ppermute | solution.py:226
  134.5 7.6 %collective-permute-done.20 = bf16[128,3456]{1,0:T(8,128)(2,1)S(1)} collective-permute-done((bf16[128,3456]{1,0:T(8,128)(2,1)S(1)}, bf16[128,3456]{1,0:T(8,128)(2,1)S(1)}, u32[]{:S(2)}, u32[]{:S(2)}) %collective-permute-start.20) | collective-permute-done | bytes 884768 | tf_op jit(solution)/shard_map/ppermute | solution.py:227
  143.8 2.3 fusion.16
  146.1 1.8 fusion.13
  149.1 3.0 %add_convert_fusion.2 = (bf16[128,3456]{1,0:T(8,128)(2,1)}, bf16[128,3456]{1,0:T(8,128)(2,1)}) fusion(bf16[128,3456]{1,0:T(8,128)(2,1)S(1)} %copy-done.25, s32[]{:T(128)S(6)} %select_n.253, bf16[1024,1152]{1,0:T(8,128)(2,1)S(1)} %fusion.4, bf16[1024,2304]{1,0:T(8,128)(2,1)} %copy-done.2, bf16[128,3456]{1,0:T(8,128)(2,1)S(1)} %copy-done.23, s32[]{:T(128)S(6)} %select_n.256), kind=kLoop, calls=%fused_computation.41 | loop fusion | flops 6193152 | bytes 10616840 | tf_op jit(solution)/shard_map/convert_element_type | solution.py:223
  152.1 1.6 collective-permute-start.21
  156.3 1.6 copy.149
  158.1 1.7 fusion.55
  161.6 11.6 %collective-permute-done.21 = bf16[128,3456]{1,0:T(8,128)(2,1)} collective-permute-done((bf16[128,3456]{1,0:T(8,128)(2,1)}, bf16[128,3456]{1,0:T(8,128)(2,1)}, u32[]{:S(2)}, u32[]{:S(2)}) %collective-permute-start.21) | collective-permute-done | bytes 884768 | tf_op jit(solution)/shard_map/ppermute | solution.py:226
  173.2 1.3 collective-permute-done.22
  176.6 1.5 convolution_convert_fusion.2
  178.1 2.4 fusion.24
  181.4 1.4 pad_maximum_fusion.terms
  182.9 1.2 copy-done.1
  184.1 44.7 %shard_map.273 = (bf16[1024,768]{1,0:T(8,128)(2,1)S(1)}, f32[256,1024]{1,0:T(8,128)S(1)}, f32[24,128]{1,0:T(8,128)S(1)}) custom-call(bf16[1024,768]{1,0:T(8,128)(2,1)S(1)} %pad_maximum_fusion.terms, f32[256,1024]{1,0:T(8,128)S(1)} %copy-done.1, f32[24,128]{1,0:T(8,128)S(1)} %pad_bitcast_fusion.vector), custom_call_target="tpu_custom_call" | custom-call | tf_op jit(solution)/shard_map/pallas_call | solution.py:486
  232.4 3.1 %add_convert_fusion.1 = (bf16[128,3456]{1,0:T(8,128)(2,1)}, bf16[128,3456]{1,0:T(8,128)(2,1)}) fusion(bf16[128,3456]{1,0:T(8,128)(2,1)} %collective-permute-done.21, s32[]{:T(128)S(6)} %select_n.250, bf16[1024,1152]{1,0:T(8,128)(2,1)S(1)} %copy-done.4, bf16[1024,2304]{1,0:T(8,128)(2,1)S(1)} %bitcast.126, bf16[128,3456]{1,0:T(8,128)(2,1)} %collective-permute-done.22, ...), kind=kLoop, calls=%fused_computation.40 | loop fusion | flops 6193152 | bytes 10616840 | tf_op jit(solution)/shard_map/convert_element_type | solution.py:223
  235.5 2.4 collective-permute-start.24
  238.9 2.5 copy.158
  243.1 1.4 fusion.21
  244.5 6.4 %collective-permute-done.24 = bf16[128,3456]{1,0:T(8,128)(2,1)} collective-permute-done((bf16[128,3456]{1,0:T(8,128)(2,1)}, bf16[128,3456]{1,0:T(8,128)(2,1)}, u32[]{:S(2)}, u32[]{:S(2)}) %collective-permute-start.24) | collective-permute-done | bytes 884768 | tf_op jit(solution)/shard_map/ppermute | solution.py:227
  251.3 1.9 convert_add_fusion.1
  (259 shorter events, 44.9 us)
Async XLA Ops:
  0.6 33.0 %copy-start = (bf16[256,1024]{1,0:T(8,128)(2,1)S(1)}, bf16[256,1024]{1,0:T(8,128)(2,1)}, u32[]{:S(2)}) copy-start(bf16[256,1024]{1,0:T(8,128)(2,1)} %param.26) | copy-start | bytes 1572868
  3.1 30.5 %collective-permute-start = (bf16[128,3456]{1,0:T(8,128)(2,1)S(1)}, bf16[128,3456]{1,0:T(8,128)(2,1)}, u32[]{:S(2)}, u32[]{:S(2)}) collective-permute-start(bf16[128,3456]{1,0:T(8,128)(2,1)S(1)} %pad_maximum_fusion.2), channel_id=1, source_target_pairs={{0,8},{8,16},{16,24},{24,28},{28,20},{20,12},{12,4},{4,0},{1,9},{9... | collective-permute-start | bytes 2654216 | tf_op jit(solution)/shard_map/ppermute | solution.py:168
  6.2 27.4 %collective-permute-start.1 = (bf16[128,3456]{1,0:T(8,128)(2,1)S(1)}, bf16[128,3456]{1,0:T(8,128)(2,1)}, u32[]{:S(2)}, u32[]{:S(2)}) collective-permute-start(bf16[128,3456]{1,0:T(8,128)(2,1)S(1)} %pad_maximum_fusion.2), channel_id=1, source_target_pairs={{8,0},{16,8},{24,16},{28,24},{20,28},{12,20},{4,12},{0,4},{9,1},{1... | collective-permute-start | bytes 2654216 | tf_op jit(solution)/shard_map/ppermute | solution.py:169
  6.5 8.0 %copy-start.46 = (s32[8]{0:T(128)S(1)}, s32[8]{0:T(128)}, u32[]{:S(2)}) copy-start(s32[8]{0:T(128)} %constant.222.clone) | copy-start | bytes 100
  7.2 16.4 %copy-start.18 = (f32[256,512]{1,0:T(8,128)}, f32[256,512]{1,0:T(8,128)S(1)}, u32[]{:S(2)}) copy-start(f32[256,512]{1,0:T(8,128)S(1)} %fusion.60) | copy-start | bytes 1572868
  7.2 16.0 %copy-start.50 = (f32[64]{0:T(128)S(1)}, f32[64]{0:T(128)}, u32[]{:S(2)}) copy-start(f32[64]{0:T(128)} %param.24) | copy-start | bytes 772
  7.2 16.3 %copy-start.54 = (f32[64]{0:T(128)S(1)}, f32[64]{0:T(128)}, u32[]{:S(2)}) copy-start(f32[64]{0:T(128)} %param.25) | copy-start | bytes 772
  24.5 9.1 %copy-start.35 = (bf16[256,4,32]{0,2,1:T(8,128)(2,1)}, bf16[256,4,32]{0,2,1:T(8,128)(2,1)S(1)}, u32[]{:S(2)}) copy-start(bf16[256,4,32]{0,2,1:T(8,128)(2,1)S(1)} %get-tuple-element.131) | copy-start | bytes 196612
  25.1 8.5 %copy-start.43 = (bf16[256,2,32]{0,2,1:T(8,128)(2,1)}, bf16[256,2,32]{0,2,1:T(8,128)(2,1)S(1)}, u32[]{:S(2)}) copy-start(bf16[256,2,32]{0,2,1:T(8,128)(2,1)S(1)} %get-tuple-element.137) | copy-start | bytes 98308
  34.0 4.1 %collective-permute-start.2 = (bf16[128,1024]{1,0:T(8,128)(2,1)S(1)}, bf16[128,1024]{1,0:T(8,128)(2,1)S(1)}, u32[]{:S(2)}, u32[]{:S(2)}) collective-permute-start(bf16[128,1024]{1,0:T(8,128)(2,1)S(1)} %dynamic-slice_convert_fusion.2), channel_id=1, source_target_pairs={{0,1},{1,0},{2,3},{3,2},{4,5},{5,4},{6,7},{7,6},{8,9},{9,8},{10,11... | collective-permute-start | bytes 786440 | tf_op jit(solution)/shard_map/ppermute | solution.py:288
  34.1 22.5 %collective-permute-start.5 = (bf16[128,3456]{1,0:T(8,128)(2,1)}, bf16[128,3456]{1,0:T(8,128)(2,1)S(1)}, u32[]{:S(2)}, u32[]{:S(2)}) collective-permute-start(bf16[128,3456]{1,0:T(8,128)(2,1)} %collective-permute-done), channel_id=1, source_target_pairs={{0,8},{8,16},{16,24},{24,28},{28,20},{20,12},{12,4},{4,0},{1,9},{9... | collective-permute-start | bytes 2654216 | tf_op jit(solution)/shard_map/ppermute | solution.py:168
  36.2 22.2 %collective-permute-start.6 = (bf16[128,3456]{1,0:T(8,128)(2,1)}, bf16[128,3456]{1,0:T(8,128)(2,1)S(1)}, u32[]{:S(2)}, u32[]{:S(2)}) collective-permute-start(bf16[128,3456]{1,0:T(8,128)(2,1)} %collective-permute-done.1), channel_id=1, source_target_pairs={{8,0},{16,8},{24,16},{28,24},{20,28},{12,20},{4,12},{0,4},{9,1},{1... | collective-permute-start | bytes 2654216 | tf_op jit(solution)/shard_map/ppermute | solution.py:169
  38.2 8.4 %collective-permute-start.3 = (bf16[128,1024]{1,0:T(8,128)(2,1)S(1)}, bf16[128,1024]{1,0:T(8,128)(2,1)S(1)}, u32[]{:S(2)}, u32[]{:S(2)}) collective-permute-start(bf16[128,1024]{1,0:T(8,128)(2,1)S(1)} %fusion.48), channel_id=1, source_target_pairs={{0,2},{1,3},{2,0},{3,1},{4,6},{5,7},{6,4},{7,5},{8,10},{9,11},{10,... | collective-permute-start | bytes 786440 | tf_op jit(solution)/shard_map/ppermute | solution.py:290
  46.7 12.1 %collective-permute-start.4 = (f32[128,1024]{1,0:T(8,128)S(1)}, f32[128,1024]{1,0:T(8,128)S(1)}, u32[]{:S(2)}, u32[]{:S(2)}) collective-permute-start(f32[128,1024]{1,0:T(8,128)S(1)} %convert_add_fusion.4), channel_id=1, source_target_pairs={{0,1},{1,0},{2,3},{3,2},{4,5},{5,4},{6,7},{7,6},{8,9},{9,8},{10,11... | collective-permute-start | bytes 1572872 | tf_op jit(solution)/shard_map/ppermute | solution.py:292
  56.6 21.3 %collective-permute-start.7 = (bf16[128,3456]{1,0:T(8,128)(2,1)S(1)}, bf16[128,3456]{1,0:T(8,128)(2,1)S(1)}, u32[]{:S(2)}, u32[]{:S(2)}) collective-permute-start(bf16[128,3456]{1,0:T(8,128)(2,1)S(1)} %collective-permute-done.5), channel_id=1, source_target_pairs={{0,8},{8,16},{16,24},{24,28},{28,20},{20,12},{12,4},{4,0},{1,9},{9... | collective-permute-start | bytes 2654216 | tf_op jit(solution)/shard_map/ppermute | solution.py:168
  58.4 21.3 %collective-permute-start.8 = (bf16[128,3456]{1,0:T(8,128)(2,1)S(1)}, bf16[128,3456]{1,0:T(8,128)(2,1)S(1)}, u32[]{:S(2)}, u32[]{:S(2)}) collective-permute-start(bf16[128,3456]{1,0:T(8,128)(2,1)S(1)} %collective-permute-done.6), channel_id=1, source_target_pairs={{8,0},{16,8},{24,16},{28,24},{20,28},{12,20},{4,12},{0,4},{9,1},{1... | collective-permute-start | bytes 2654216 | tf_op jit(solution)/shard_map/ppermute | solution.py:169
  77.9 11.0 %collective-permute-start.9 = (bf16[64,3456]{1,0:T(8,128)(2,1)S(1)}, bf16[64,3456]{1,0:T(8,128)(2,1)S(1)}, u32[]{:S(2)}, u32[]{:S(2)}) collective-permute-start(bf16[64,3456]{1,0:T(8,128)(2,1)S(1)} %slice.117), channel_id=1, source_target_pairs={{0,8},{8,16},{16,24},{24,28},{28,20},{20,12},{12,4},{4,0},{1,9},{9... | collective-permute-start | bytes 1327112 | tf_op jit(solution)/shard_map/ppermute | solution.py:182
  79.7 10.8 %copy-start.42 = (f32[1024]{0:T(1024)S(1)}, f32[1024]{0:T(1024)}, u32[]{:S(2)}) copy-start(f32[1024]{0:T(1024)} %param.27) | copy-start | bytes 12292
  79.7 10.8 %collective-permute-start.10 = (bf16[64,3456]{1,0:T(8,128)(2,1)S(1)}, bf16[64,3456]{1,0:T(8,128)(2,1)S(1)}, u32[]{:S(2)}, u32[]{:S(2)}) collective-permute-start(bf16[64,3456]{1,0:T(8,128)(2,1)S(1)} %slice.118), channel_id=1, source_target_pairs={{8,0},{16,8},{24,16},{28,24},{20,28},{12,20},{4,12},{0,4},{9,1},{1... | collective-permute-start | bytes 1327112 | tf_op jit(solution)/shard_map/ppermute | solution.py:183
  96.2 17.8 %copy-start.2 = (bf16[1024,2304]{1,0:T(8,128)(2,1)}, bf16[1024,2304]{1,0:T(8,128)(2,1)S(1)}, u32[]{:S(2)}) copy-start(bf16[1024,2304]{1,0:T(8,128)(2,1)S(1)} %convolution_convert_fusion) | copy-start | bytes 14155780
  97.1 51.9 %copy-start.3 = (bf16[1024,1152]{1,0:T(8,128)(2,1)}, bf16[1024,1152]{1,0:T(8,128)(2,1)S(1)}, u32[]{:S(2)}) copy-start(bf16[1024,1152]{1,0:T(8,128)(2,1)S(1)} %fusion.4) | copy-start | bytes 7077892
  98.1 4.6 %collective-permute-start.14 = (bf16[128,1024]{1,0:T(8,128)(2,1)S(1)}, bf16[128,1024]{1,0:T(8,128)(2,1)S(1)}, u32[]{:S(2)}, u32[]{:S(2)}) collective-permute-start(bf16[128,1024]{1,0:T(8,128)(2,1)S(1)} %dynamic-slice_convert_fusion), channel_id=1, source_target_pairs={{0,1},{1,0},{2,3},{3,2},{4,5},{5,4},{6,7},{7,6},{8,9},{9,8},{10,11... | collective-permute-start | bytes 786440 | tf_op jit(solution)/shard_map/ppermute | solution.py:288
  98.2 2.8 %collective-permute-start.11 = (bf16[128,1024]{1,0:T(8,128)(2,1)S(1)}, bf16[128,1024]{1,0:T(8,128)(2,1)S(1)}, u32[]{:S(2)}, u32[]{:S(2)}) collective-permute-start(bf16[128,1024]{1,0:T(8,128)(2,1)S(1)} %dynamic-slice_convert_fusion.1), channel_id=1, source_target_pairs={{0,1},{1,0},{2,3},{3,2},{4,5},{5,4},{6,7},{7,6},{8,9},{9,8},{10,11... | collective-permute-start | bytes 786440 | tf_op jit(solution)/shard_map/ppermute | solution.py:288
  98.9 12.2 %collective-permute-start.15 = (bf16[64,3456]{1,0:T(8,128)(2,1)S(1)}, bf16[64,3456]{1,0:T(8,128)(2,1)S(1)}, u32[]{:S(2)}, u32[]{:S(2)}) collective-permute-start(bf16[64,3456]{1,0:T(8,128)(2,1)S(1)} %get-tuple-element.114), channel_id=1, source_target_pairs={{0,8},{8,16},{16,24},{24,28},{28,20},{20,12},{12,4},{4,0},{1,9},{9... | collective-permute-start | bytes 1327112 | tf_op jit(solution)/shard_map/ppermute | solution.py:226
  100.5 11.8 %collective-permute-start.16 = (bf16[64,3456]{1,0:T(8,128)(2,1)S(1)}, bf16[64,3456]{1,0:T(8,128)(2,1)S(1)}, u32[]{:S(2)}, u32[]{:S(2)}) collective-permute-start(bf16[64,3456]{1,0:T(8,128)(2,1)S(1)} %get-tuple-element.115), channel_id=1, source_target_pairs={{8,0},{16,8},{24,16},{28,24},{20,28},{12,20},{4,12},{0,4},{9,1},{1... | collective-permute-start | bytes 1327112 | tf_op jit(solution)/shard_map/ppermute | solution.py:227
  101.1 18.6 %collective-permute-start.12 = (bf16[128,1024]{1,0:T(8,128)(2,1)S(1)}, bf16[128,1024]{1,0:T(8,128)(2,1)S(1)}, u32[]{:S(2)}, u32[]{:S(2)}) collective-permute-start(bf16[128,1024]{1,0:T(8,128)(2,1)S(1)} %fusion.49), channel_id=1, source_target_pairs={{0,2},{1,3},{2,0},{3,1},{4,6},{5,7},{6,4},{7,5},{8,10},{9,11},{10,... | collective-permute-start | bytes 786440 | tf_op jit(solution)/shard_map/ppermute | solution.py:290
  112.4 7.1 %collective-permute-start.17 = (bf16[128,1024]{1,0:T(8,128)(2,1)S(1)}, bf16[128,1024]{1,0:T(8,128)(2,1)S(1)}, u32[]{:S(2)}, u32[]{:S(2)}) collective-permute-start(bf16[128,1024]{1,0:T(8,128)(2,1)S(1)} %convert_element_type.223), channel_id=1, source_target_pairs={{0,2},{1,3},{2,0},{3,1},{4,6},{5,7},{6,4},{7,5},{8,10},{9,11},{10,... | collective-permute-start | bytes 786440 | tf_op jit(solution)/shard_map/ppermute | solution.py:290
  114.3 20.2 %collective-permute-start.19 = (bf16[128,3456]{1,0:T(8,128)(2,1)S(1)}, bf16[128,3456]{1,0:T(8,128)(2,1)S(1)}, u32[]{:S(2)}, u32[]{:S(2)}) collective-permute-start(bf16[128,3456]{1,0:T(8,128)(2,1)S(1)} %pad_maximum_fusion.3), channel_id=1, source_target_pairs={{0,8},{8,16},{16,24},{24,28},{28,20},{20,12},{12,4},{4,0},{1,9},{9... | collective-permute-start | bytes 2654216 | tf_op jit(solution)/shard_map/ppermute | solution.py:226
  119.6 2.0 collective-permute-start.18
  119.8 2.5 collective-permute-start.13
  120.4 21.6 %collective-permute-start.20 = (bf16[128,3456]{1,0:T(8,128)(2,1)S(1)}, bf16[128,3456]{1,0:T(8,128)(2,1)S(1)}, u32[]{:S(2)}, u32[]{:S(2)}) collective-permute-start(bf16[128,3456]{1,0:T(8,128)(2,1)S(1)} %pad_maximum_fusion.4), channel_id=1, source_target_pairs={{8,0},{16,8},{24,16},{28,24},{20,28},{12,20},{4,12},{0,4},{9,1},{1... | collective-permute-start | bytes 2654216 | tf_op jit(solution)/shard_map/ppermute | solution.py:227
  125.3 16.8 %copy-start.34 = (bf16[256,256]{0,1:T(8,128)(2,1)}, bf16[256,256]{0,1:T(8,128)(2,1)S(1)}, u32[]{:S(2)}) copy-start(bf16[256,256]{0,1:T(8,128)(2,1)S(1)} %convolution_convert_fusion.4) | copy-start | bytes 393220
  149.1 9.0 %copy-start.49 = (f32[512]{0:T(512)S(1)}, f32[512]{0:T(512)}, u32[]{:S(2)}) copy-start(f32[512]{0:T(512)} %rsqrt.45) | copy-start | bytes 6148
  152.1 7.7 %copy-start.33 = (f32[256,128]{1,0:T(8,128)S(1)}, f32[256,128]{1,0:T(8,128)}, u32[]{:S(2)}) copy-start(f32[256,128]{1,0:T(8,128)} %copy.143) | copy-start | bytes 393220
  152.1 8.4 %copy-start.15 = (bf16[2,2,256,256]{2,3,1,0:T(8,128)(2,1)S(1)}, bf16[2,2,256,256]{2,3,1,0:T(8,128)(2,1)}, u32[]{:S(2)}) copy-start(bf16[2,2,256,256]{2,3,1,0:T(8,128)(2,1)} %copy-done.14) | copy-start | bytes 1572868
  152.1 23.2 %copy-start.12 = (f32[256,256]{0,1:T(8,128)S(1)}, f32[256,256]{0,1:T(8,128)}, u32[]{:S(2)}) copy-start(f32[256,256]{0,1:T(8,128)} %copy-done.11) | copy-start | bytes 786436
  152.1 21.1 %collective-permute-start.21 = (bf16[128,3456]{1,0:T(8,128)(2,1)}, bf16[128,3456]{1,0:T(8,128)(2,1)}, u32[]{:S(2)}, u32[]{:S(2)}) collective-permute-start(bf16[128,3456]{1,0:T(8,128)(2,1)} %get-tuple-element.112), channel_id=1, source_target_pairs={{0,8},{8,16},{16,24},{24,28},{28,20},{20,12},{12,4},{4,0},{1,9},{9... | collective-permute-start | bytes 2654216 | tf_op jit(solution)/shard_map/ppermute | solution.py:226
  153.8 20.8 %collective-permute-start.22 = (bf16[128,3456]{1,0:T(8,128)(2,1)}, bf16[128,3456]{1,0:T(8,128)(2,1)}, u32[]{:S(2)}, u32[]{:S(2)}) collective-permute-start(bf16[128,3456]{1,0:T(8,128)(2,1)} %get-tuple-element.111), channel_id=1, source_target_pairs={{8,0},{16,8},{24,16},{28,24},{20,28},{12,20},{4,12},{0,4},{9,1},{1... | collective-permute-start | bytes 2654216 | tf_op jit(solution)/shard_map/ppermute | solution.py:227
  158.1 18.3 %copy-start.21 = (f32[256,256]{1,0:T(8,128)S(1)}, f32[256,256]{1,0:T(8,128)}, u32[]{:S(2)}) copy-start(f32[256,256]{1,0:T(8,128)} %copy.136) | copy-start | bytes 786436
  159.8 16.6 %copy-start.51 = (f32[256]{0:T(256)S(1)}, f32[256]{0:T(256)}, u32[]{:S(2)}) copy-start(f32[256]{0:T(256)} %mul.682) | copy-start | bytes 3076
  160.5 16.0 %copy-start.45 = (bf16[256,128]{1,0:T(8,128)(2,1)}, bf16[256,128]{1,0:T(8,128)(2,1)S(1)}, u32[]{:S(2)}) copy-start(bf16[256,128]{1,0:T(8,128)(2,1)S(1)} %fusion.64) | copy-start | bytes 196612
  160.5 16.0 %copy-start.44 = (bf16[256,128]{1,0:T(8,128)(2,1)S(1)}, bf16[256,128]{1,0:T(8,128)(2,1)}, u32[]{:S(2)}) copy-start(bf16[256,128]{1,0:T(8,128)(2,1)} %copy.149) | copy-start | bytes 196612
  160.6 16.0 %copy-start.53 = (f32[256]{0:T(256)S(1)}, f32[256]{0:T(256)}, u32[]{:S(2)}) copy-start(f32[256]{0:T(256)} %copy-done.52) | copy-start | bytes 3076
  181.4 47.4 %copy-start.9 = (bf16[256,1024]{1,0:T(8,128)(2,1)S(1)}, bf16[256,1024]{1,0:T(8,128)(2,1)}, u32[]{:S(2)}) copy-start(bf16[256,1024]{1,0:T(8,128)(2,1)} %param.18) | copy-start | bytes 1572868
  181.4 49.6 %slice-start = ((s8[4718592]{0:T(1024)(128)(4,1)}), s8[524288]{0:T(1024)(128)(4,1)S(1)}, s32[]{:S(2)}) async-start(s8[4718592]{0:T(1024)(128)(4,1)} %bitcast.125), calls=%async_computation | async-start | bytes 1048576
  235.5 15.4 %collective-permute-start.24 = (bf16[128,3456]{1,0:T(8,128)(2,1)}, bf16[128,3456]{1,0:T(8,128)(2,1)}, u32[]{:S(2)}, u32[]{:S(2)}) collective-permute-start(bf16[128,3456]{1,0:T(8,128)(2,1)} %get-tuple-element.110), channel_id=1, source_target_pairs={{8,0},{16,8},{24,16},{28,24},{20,28},{12,20},{4,12},{0,4},{9,1},{1... | collective-permute-start | bytes 2654216 | tf_op jit(solution)/shard_map/ppermute | solution.py:227
  237.9 13.4 %collective-permute-start.23 = (bf16[128,3456]{1,0:T(8,128)(2,1)}, bf16[128,3456]{1,0:T(8,128)(2,1)}, u32[]{:S(2)}, u32[]{:S(2)}) collective-permute-start(bf16[128,3456]{1,0:T(8,128)(2,1)} %get-tuple-element.109), channel_id=1, source_target_pairs={{0,8},{8,16},{16,24},{24,28},{28,20},{20,12},{12,4},{4,0},{1,9},{9... | collective-permute-start | bytes 2654216 | tf_op jit(solution)/shard_map/ppermute | solution.py:226
  243.1 8.2 %copy-start.5 = (bf16[1024,1152]{1,0:T(8,128)(2,1)S(1)}, bf16[1024,1152]{1,0:T(8,128)(2,1)}, u32[]{:S(2)}) copy-start(bf16[1024,1152]{1,0:T(8,128)(2,1)} %copy-done.3) | copy-start | bytes 7077892
  (37 other events, 146.6 us)
